TPU v7x, 32 devices: a whole 2x2x4 slice. The times are simulated.
32 devices in a mesh: row: 8 (over z, x), col: 4 (over y, core).
Axes of the slice: x: 2, y: 2, z: 4, core: 2. Of those that a mesh axis runs over, the one named last changes fastest.
Arguments:
- tiles: bfloat16 [8, 4, 32, 128, 128], P('row', 'col'), may hold values from -0.375 to 0.375
- coords: int32 [8, 4, 32, 2], P('row', 'col'), may hold values from 0 to 8191, as said below
- counts: int32 [8, 4], P('row', 'col'), may hold values from 16 to 32, as said below
- rhs: float32 [2, 4194304], P(None, ('row', 'col')), may hold values from -50 to 50
Outputs:
- solution: float32 [2, 4194304], P(None, ('col', 'row'))
- phi_bar: float32 [2], replicated
Inputs may be any that keep to these rules, and one draw needn't show every extreme that they name: coords[p, q, k, 0] is a local block row below 4096 and coords[p, q, k, 1] a local block column below 8192; within one tile no two slots share a block row and no two share a block column; counting all 32 slots of a tile, exactly 8 of its block rows fall in each of the 4 ranges of 1024 consecutive block rows, and exactly 4 of its block columns in each of the 8 ranges of 1024 consecutive block columns. The first counts[p, q] slots of tile (p, q) are used; some tile uses all 32.
All inputs are finite; a program needn't handle non-finite values.
Results may differ from a plain program's by a relative error of at most 0.015.
Values may be sent and summed in bfloat16 or wider, within the bound.
A program may use at most 192 MiB of HBM per device.

v0:
```python
import jax
import jax.numpy as jnp
from jax import lax
from jax.sharding import PartitionSpec as P

ITERS = 2


EPS = 1e-06


def rounded(values):
    return lax.optimization_barrier(values.astype(jnp.bfloat16))


def select_blocks(piece, block_ids, block):
    width = piece.shape[1]
    offsets = block_ids[:, None] * block + jnp.arange(block, dtype=jnp.int32)[None, :]
    inside = (offsets >= 0) & (offsets < width)
    clipped = jnp.clip(offsets, 0, width - 1)
    taken = jnp.take(piece, clipped.reshape(-1), axis=1).reshape(
        piece.shape[0], block_ids.shape[0], block
    )
    taken = jnp.where(inside[None, :, :], taken, jnp.zeros_like(taken))
    values = piece.astype(jnp.float32)
    return (taken, jnp.sum(values * values, axis=1))


def forward_products(picked, tile_data):
    return jnp.einsum("rkc,kdc->krd", picked, tile_data, preferred_element_type=jnp.float32)


def adjoint_products(picked, tile_data):
    return jnp.einsum("rkd,kdc->krc", picked, tile_data, preferred_element_type=jnp.float32)


def bucket_blocks(products, block_ids, valid, range_len, owners):
    slot_count = block_ids.shape[0]
    capacity = slot_count // owners
    values = rounded(products * valid[:, None, None])
    owner_ids = block_ids // range_len
    local_ids = block_ids % range_len
    slot_index = jnp.arange(slot_count, dtype=jnp.int32)
    live = valid > 0.5
    earlier = (
        (owner_ids[:, None] == owner_ids[None, :])
        & live[None, :]
        & (slot_index[None, :] < slot_index[:, None])
    )
    position = jnp.sum(earlier.astype(jnp.int32), axis=1)
    target = owner_ids * capacity + position
    onehot = (target[None, :] == jnp.arange(owners * capacity, dtype=jnp.int32)[:, None]) & live[
        None, :
    ]
    sent = jnp.einsum(
        "ek,krd->erd", onehot.astype(jnp.bfloat16), values, preferred_element_type=jnp.float32
    ).astype(jnp.bfloat16)
    sent = sent.reshape(owners, capacity, values.shape[1], values.shape[2])
    labels = jnp.sum(jnp.where(onehot, local_ids[None, :] + 1, 0), axis=1).reshape(owners, capacity)
    return (sent, labels)


def place_blocks(received, labels, range_len):
    flat = received.reshape(-1, received.shape[2], received.shape[3])
    flat_labels = labels.reshape(-1)
    placing = (
        flat_labels[None, :] == jnp.arange(1, range_len + 1, dtype=jnp.int32)[:, None]
    ).astype(jnp.bfloat16)
    summed = jnp.einsum("bk,krd->rbd", placing, flat, preferred_element_type=jnp.float32)
    return summed.reshape(flat.shape[1], range_len * flat.shape[2])


def on_device(tiles, coords, counts, rhs):
    tile_data = tiles[0, 0]
    row_ids = coords[0, 0, :, 0]
    col_ids = coords[0, 0, :, 1]
    slot_count = tile_data.shape[0]
    block = tile_data.shape[1]
    valid = (jnp.arange(slot_count, dtype=jnp.int32) < counts[0, 0]).astype(jnp.float32)
    realizations = rhs.shape[0]
    piece_len = rhs.shape[1]
    range_len = piece_len // block

    def fold_rows(piece):
        return select_blocks(piece, row_ids, block)

    def fold_cols(piece):
        return select_blocks(piece, col_ids, block)

    def gather_u(u_rounded):
        return fold_rows(lax.all_gather(u_rounded, "col", axis=1, tiled=True))

    def gather_v(v_rounded):
        return fold_cols(lax.all_gather(v_rounded, "row", axis=1, tiled=True))

    def own_norm(vector_bf):
        values = vector_bf.astype(jnp.float32)
        return jnp.sqrt(lax.psum(jnp.sum(values * values, axis=1), ("row", "col")) + EPS)

    def u_norm(u_rounded):
        return own_norm(u_rounded)

    def v_norm(v_piece):
        return own_norm(v_piece)

    def forward_sum(picked_v):
        products = forward_products(picked_v, tile_data)
        sent, labels = bucket_blocks(products, row_ids, valid, range_len, lax.axis_size("col"))
        received, got_labels = (
            lax.all_to_all(sent, "col", split_axis=0, concat_axis=0, tiled=True),
            lax.all_to_all(labels, "col", split_axis=0, concat_axis=0, tiled=True),
        )
        return place_blocks(received, got_labels, range_len)

    def adjoint(picked_u, beta_now, v_former):
        products = adjoint_products(picked_u, tile_data)
        sent, labels = bucket_blocks(products, col_ids, valid, range_len, lax.axis_size("row"))
        received, got_labels = (
            lax.all_to_all(sent, "row", split_axis=0, concat_axis=0, tiled=True),
            lax.all_to_all(labels, "row", split_axis=0, concat_axis=0, tiled=True),
        )
        summed = place_blocks(received, got_labels, range_len)
        v_rounded = rounded(summed / beta_now[:, None] - beta_now[:, None] * v_former)
        picked_v, squares = gather_v(v_rounded)
        return (v_rounded, v_rounded, picked_v, squares)

    u_rounded = rounded(rhs)
    picked_u, u_squares = gather_u(u_rounded)
    beta_now = u_norm(u_rounded)
    u_unit = u_rounded.astype(jnp.float32) / beta_now[:, None]
    v_store, v_piece, picked_v, v_squares = adjoint(picked_u, beta_now, jnp.zeros((), jnp.float32))
    alpha_now = v_norm(v_piece)
    v_unit = v_store.astype(jnp.float32) / alpha_now[:, None]
    direction = v_piece.astype(jnp.float32) / alpha_now[:, None]
    solution = jnp.zeros((realizations, piece_len), jnp.float32)
    phi_bar = beta_now
    rho_bar = alpha_now
    for step in range(ITERS):
        final_turn = step + 1 == ITERS
        summed = forward_sum(picked_v)
        u_rounded = rounded(summed / alpha_now[:, None] - alpha_now[:, None] * u_unit)
        if final_turn:
            beta_now = u_norm(u_rounded)
        else:
            picked_u, u_squares = gather_u(u_rounded)
            beta_now = u_norm(u_rounded)
        rho_value = jnp.sqrt(rho_bar * rho_bar + beta_now * beta_now)
        cosine = rho_bar / rho_value
        sine = beta_now / rho_value
        phi_value = cosine * phi_bar
        phi_bar = sine * phi_bar
        solution = solution + (phi_value / rho_value)[:, None] * direction
        u_unit = u_rounded.astype(jnp.float32) / beta_now[:, None]
        if not final_turn:
            v_store, v_piece, picked_v, v_squares = adjoint(picked_u, beta_now, v_unit)
            alpha_now = v_norm(v_piece)
            theta_value = sine * alpha_now
            rho_bar = -cosine * alpha_now
            v_unit = v_store.astype(jnp.float32) / alpha_now[:, None]
            piece_unit = v_piece.astype(jnp.float32) / alpha_now[:, None]
            direction = piece_unit - (theta_value / rho_value)[:, None] * direction
    return (solution, phi_bar)


def solution(mesh):
    return jax.shard_map(
        on_device,
        mesh=mesh,
        in_specs=(
            P("row", "col", None, None, None),
            P("row", "col", None, None),
            P("row", "col"),
            P(None, ("row", "col")),
        ),
        out_specs=(P(None, ("col", "row")), P()),
        check_vma=False,
    )
```

profile of v0, /device:TPU:0, one launch (start us, length us, event | category | flops | bytes accessed | tf_op | source)
XLA Modules:
  0.0 980.7 jit_solution(2554390079752002479)
XLA Ops:
  7.2 2.5 convert_element_type.88
  10.4 0.7 fusion.88
  11.1 0.8 bitcast_multiply_fusion
  11.8 0.7 and_select_fusion.1
  12.8 0.7 all_to_all.27
  13.5 2.2 fusion.9
  15.8 7.3 all-to-all-start.1
  23.0 40.8 %psum.35 = f32[2]{0:T(128)S(1)} all-reduce(f32[2]{0:T(128)S(1)} %fusion.9), channel_id=1, replica_groups=mesh['row'=8,'col'=4] {'row','col'}, use_global_device_ids=true, to_apply=%region_3.5 | all-reduce | flops 2 | bytes 16 | tf_op jit(solution)/shard_map/psum | solution.py:98
  64.1 78.6 %copy.56 = bf16[2,524288]{0,1:T(8,128)(2,1)} copy(bf16[2,524288]{1,0:T(2,128)(2,1)} %all-gather.5.cloned.1.call-done) | data formatting | bytes 4194304 | tf_op jit(solution)/shard_map/all_gather | solution.py:91
  142.7 43.6 %gather_fusion = bf16[4096,2]{1,0:T(8,128)(2,1)S(1)} fusion(bf16[2,524288]{0,1:T(8,128)(2,1)} %copy.56, s32[4096]{0:T(1024)S(1)} %fusion.57), kind=kCustom, calls=%fused_computation.clone | custom fusion | bytes 49152 | tf_op jit(solution)/shard_map/jit(_take)/gather | solution.py:21
  186.3 2.1 broadcast_select_fusion.1
  190.0 5.3 all-to-all-start
  195.9 0.7 reduce.6
  196.6 5.3 all-to-all-done
  202.6 1.7 fusion.18
  204.3 0.7 all_to_all.30
  205.0 3.2 all-to-all-start.3
  208.5 3.4 all-to-all-done.3
  211.9 0.7 reduce.7
  212.5 2.2 fusion.10
  214.8 39.9 %psum.36 = f32[2]{0:T(128)S(1)} all-reduce(f32[2]{0:T(128)S(1)} %fusion.10), channel_id=1, replica_groups=mesh['row'=8,'col'=4] {'row','col'}, use_global_device_ids=true, to_apply=%region_5.7 | all-reduce | flops 2 | bytes 16 | tf_op jit(solution)/shard_map/psum | solution.py:98
  254.8 20.4 %all-gather.7.cloned.1.call-done = bf16[2,1048576]{1,0:T(2,128)(2,1)} async-done(((bf16[2,131072]{1,0:T(2,128)(2,1)}), bf16[2,1048576]{1,0:T(2,128)(2,1)}) %all-gather.7.cloned.1.call-update) | async-done | bytes 4194320 | tf_op jit(solution)/shard_map/all_gather | solution.py:94
  275.2 176.7 %gather_fusion.1 = bf16[4096,2]{0,1:T(2,128)(2,1)S(1)} fusion(bf16[2,1048576]{1,0:T(2,128)(2,1)} %all-gather.7.cloned.1.call-done, s32[4096]{0:T(1024)S(1)} %fusion.52), kind=kCustom, calls=%fused_computation.1.clone | custom fusion | bytes 49152 | tf_op jit(solution)/shard_map/jit(_take)/gather | solution.py:21
  453.2 3.3 all-to-all-start.2
  456.7 3.6 all-to-all-done.2
  460.7 1.3 copy.68
  462.0 3.1 fusion.19
  465.1 2.2 fusion.11
  467.3 38.5 %psum.37 = f32[2]{0:T(128)S(1)} all-reduce(f32[2]{0:T(128)S(1)} %fusion.11), channel_id=1, replica_groups=mesh['row'=8,'col'=4] {'row','col'}, use_global_device_ids=true, to_apply=%region_9.12 | all-reduce | flops 2 | bytes 16 | tf_op jit(solution)/shard_map/psum | solution.py:98
  505.8 78.6 %copy.69 = bf16[2,524288]{0,1:T(8,128)(2,1)} copy(bf16[2,524288]{1,0:T(2,128)(2,1)} %all-gather.9.cloned.1.call-done) | data formatting | bytes 4194304 | tf_op jit(solution)/shard_map/all_gather | solution.py:91
  584.4 62.7 %gather_fusion.2 = bf16[4096,2]{1,0:T(8,128)(2,1)} fusion(bf16[2,524288]{0,1:T(8,128)(2,1)} %copy.69, s32[4096]{0:T(1024)S(1)} %fusion.57), kind=kCustom, calls=%fused_computation.2.clone | custom fusion | bytes 49152 | tf_op jit(solution)/shard_map/jit(_take)/gather | solution.py:21
  647.1 3.4 broadcast_select_fusion
  652.0 5.3 all-to-all-start.4
  657.4 6.5 all-to-all-done.4
  664.2 1.3 copy.74
  665.5 3.3 fusion.21
  668.9 2.3 fusion.12
  671.2 39.7 %psum.38 = f32[2]{0:T(128)S(1)} all-reduce(f32[2]{0:T(128)S(1)} %fusion.12), channel_id=1, replica_groups=mesh['row'=8,'col'=4] {'row','col'}, use_global_device_ids=true, to_apply=%region_11.14 | all-reduce | flops 2 | bytes 16 | tf_op jit(solution)/shard_map/psum | solution.py:98
  710.8 29.9 %all-gather.11.cloned.1.call-done = bf16[2,1048576]{1,0:T(2,128)(2,1)} async-done(((bf16[2,131072]{1,0:T(2,128)(2,1)}), bf16[2,1048576]{1,0:T(2,128)(2,1)}) %all-gather.11.cloned.1.call-update) | async-done | bytes 4194320 | tf_op jit(solution)/shard_map/all_gather | solution.py:94
  740.8 176.7 %gather_fusion.3 = bf16[4096,2]{0,1:T(2,128)(2,1)S(1)} fusion(bf16[2,1048576]{1,0:T(2,128)(2,1)} %all-gather.11.cloned.1.call-done, s32[4096]{0:T(1024)S(1)} %fusion.52), kind=kCustom, calls=%fused_computation.3.clone | custom fusion | bytes 49152 | tf_op jit(solution)/shard_map/jit(_take)/gather | solution.py:21
  918.8 3.5 all-to-all-start.5
  922.3 3.6 all-to-all-done.5
  925.9 1.3 convolution_bitcast_fusion
  927.2 2.5 copy.79
  929.8 2.3 fusion.20
  932.1 1.2 multiply_reduce_fusion
  933.3 38.3 %psum.39 = f32[2]{0:T(128)S(1)} all-reduce(f32[2]{0:T(128)S(1)} %multiply_reduce_fusion), channel_id=1, replica_groups=mesh['row'=8,'col'=4] {'row','col'}, use_global_device_ids=true, to_apply=%region_13.16 | all-reduce | flops 2 | bytes 16 | tf_op jit(solution)/shard_map/psum | solution.py:98
  972.1 2.0 multiply_add_fusion
  (62 shorter events, 9.7 us)
Async XLA Ops:
  7.2 181.7 %copy-start = (bf16[1,1,32,128,128]{4,3,2,1,0:T(8,128)(2,1)S(1)}, bf16[1,1,32,128,128]{4,3,2,1,0:T(8,128)(2,1)}, u32[]{:S(2)}) copy-start(bf16[1,1,32,128,128]{4,3,2,1,0:T(8,128)(2,1)} %param.8) | copy-start | bytes 3145732
  7.2 56.9 %all-gather.5.cloned.1.call-start = ((), (), s32[]{:S(2)}) async-start(), calls=%async_computation.6 | async-start | bytes 2621440 | tf_op jit(solution)/shard_map/all_gather | solution.py:91
  15.8 174.2 %all-to-all-start.1 = ((s32[8,1,4]{2,1,0:T(1,128)}), s32[8,1,4]{2,1,0:T(1,128)S(1)}, u32[]{:S(2)}, u32[]{:S(2)}) async-start(s32[8,1,4]{2,1,0:T(1,128)} %bitcast.10), calls=%async_computation.1 | async-start | bytes 8192 | tf_op jit(solution)/shard_map/all_to_all | solution.py:120
  190.0 11.9 %all-to-all-start = ((bf16[8,4,2,128]{3,1,2,0:T(4,128)(2,1)}), bf16[8,4,2,128]{3,1,2,0:T(4,128)(2,1)S(1)}, u32[]{:S(2)}, u32[]{:S(2)}) async-start(bf16[8,4,2,128]{3,1,2,0:T(4,128)(2,1)} %copy.59), calls=%async_computation | async-start | bytes 32768 | tf_op jit(solution)/shard_map/all_to_all | solution.py:119
  195.3 79.8 %all-gather.7.cloned.1.call-start = ((), (), s32[]{:S(2)}) async-start(), calls=%async_computation.7 | async-start | bytes 4718592 | tf_op jit(solution)/shard_map/all_gather | solution.py:94
  204.3 257.7 %copy-start.1 = (bf16[2,131072]{1,0:T(2,128)(2,1)S(1)}, bf16[2,131072]{1,0:T(2,128)(2,1)}, u32[]{:S(2)}) copy-start(bf16[2,131072]{1,0:T(2,128)(2,1)} %convert_element_type.88) | copy-start | bytes 1572868
  205.0 6.9 all-to-all-start.3
  453.2 7.1 all-to-all-start.2
  456.5 49.3 %all-gather.9.cloned.1.call-start = ((), (), s32[]{:S(2)}) async-start(), calls=%async_computation.8 | async-start | bytes 2621440 | tf_op jit(solution)/shard_map/all_gather | solution.py:91
  584.4 81.2 %copy-start.2 = (bf16[2,131072]{1,0:T(2,128)(2,1)S(1)}, bf16[2,131072]{1,0:T(2,128)(2,1)}, u32[]{:S(2)}) copy-start(bf16[2,131072]{1,0:T(2,128)(2,1)} %fusion.18) | copy-start | bytes 1572868
  652.0 11.9 %all-to-all-start.4 = ((bf16[8,4,2,128]{3,1,2,0:T(4,128)(2,1)}), bf16[8,4,2,128]{3,1,2,0:T(4,128)(2,1)S(1)}, u32[]{:S(2)}, u32[]{:S(2)}) async-start(bf16[8,4,2,128]{3,1,2,0:T(4,128)(2,1)} %copy.72), calls=%async_computation.4 | async-start | bytes 32768 | tf_op jit(solution)/shard_map/all_to_all | solution.py:119
  657.3 83.5 %all-gather.11.cloned.1.call-start = ((), (), s32[]{:S(2)}) async-start(), calls=%async_computation.9 | async-start | bytes 4718592 | tf_op jit(solution)/shard_map/all_gather | solution.py:94
  668.8 260.9 %copy-start.3 = (bf16[2,131072]{1,0:T(2,128)(2,1)S(1)}, bf16[2,131072]{1,0:T(2,128)(2,1)}, u32[]{:S(2)}) copy-start(bf16[2,131072]{1,0:T(2,128)(2,1)} %fusion.19) | copy-start | bytes 1572868
  710.8 261.3 %copy-start.4 = (bf16[2,131072]{1,0:T(2,128)(2,1)S(1)}, bf16[2,131072]{1,0:T(2,128)(2,1)}, u32[]{:S(2)}) copy-start(bf16[2,131072]{1,0:T(2,128)(2,1)} %get-tuple-element.18) | copy-start | bytes 1572868
  918.8 7.1 all-to-all-start.5
Sparse Core Ops, SparseCore 0:
  9.8 25.8 all-gather.4
  204.4 70.6 all-gather.6
  465.2 20.8 all-gather.8
  669.0 71.7 all-gather.10
where the time goes:
time: 991 us; the launch traced here: 981 us
  local copies, waits for them, and re-layouts  628 us (63%)
  blocking collectives  197 us (20%)
  waiting for transfers between devices  72.7 us (7%)
  other arithmetic  35.4 us (4%)
  starting transfers between devices  28.2 us (3%)
  between operations  14.6 us (1%)
    gather x4, local copies, waits for them, and re-layouts, select_blocks(): jnp.take(piece, clipped.reshape(-1), axis=1)  460 us
    psum x5, blocking collectives, own_norm(): lax.psum(jnp.sum(values * values, axis=1), ('row', 'col')) + EPS  197 us
    all_gather x2, local copies, waits for them, and re-layouts, gather_u(): return fold_rows(lax.all_gather(u_rounded, 'col', axis=1, tiled=True))  157 us
    all_gather x2, waiting for transfers between devices, gather_v(): return fold_cols(lax.all_gather(v_rounded, 'row', axis=1, tiled=True))  50.3 us
  transfers between devices with their start and end apart: 10, of which 7 were waited for; matrix products, arithmetic and copies ran while one was open for 14% of the time, Pallas kernels for 0%

commit v1 on v0

v1 whole, which is shorter than its diff:
```python
import functools

import jax
import jax.numpy as jnp
from jax import lax
from jax.experimental import pallas as pl
from jax.experimental.pallas import tpu as pltpu
from jax.sharding import PartitionSpec as P

EPS = 1e-06
LANES = 128
BF = jnp.bfloat16
F32 = jnp.float32


def iota(shape, dim):
    return lax.broadcasted_iota(jnp.int32, shape, dim)


def diagonal_dot(values, stacked, slots):
    row_slot = iota(values.shape, 0) % slots
    wide = jnp.concatenate(
        [jnp.where(row_slot == k, values, 0.0).astype(BF) for k in range(slots)], axis=1
    )
    return jnp.dot(wide, stacked, preferred_element_type=F32)


def per_realization(products, rows):
    total = jnp.sum(products.reshape(-1, rows, LANES), axis=0)
    half = rows // 2
    lanes = [jnp.sum(total[r * half : (r + 1) * half], axis=0, keepdims=True) for r in range(2)]
    return [jnp.sum(lane, axis=1, keepdims=True) for lane in lanes]


def solver(
    nr, nc, slots, range_len,
    coords, counts, tiles_hbm, rhs_hbm,
    out_ref, phi_ref,
    rhs_v, ub, tiles_v, tt, row_ids, col_ids, picks_out, picks_in, c0, c1, d0, d1,
    stats_col, stats_row, m_col, m_full, sub_full, place,
    load_sem, send_col, recv_col, send_row, recv_row,
):
    me_p = lax.axis_index("row")
    me_q = lax.axis_index("col")
    rows = 2 * slots
    per = LANES // slots

    load_rhs = pltpu.make_async_copy(rhs_hbm, rhs_v, load_sem.at[0])
    load_tiles = pltpu.make_async_copy(tiles_hbm, tiles_v, load_sem.at[1])
    load_rhs.start()
    load_tiles.start()

    def row_peer(o):
        return (lax.rem(me_p + o, nr), me_q)

    def col_peer(o):
        return (me_p, lax.rem(me_q + o, nc))

    barrier = pltpu.get_barrier_semaphore()
    for o in range(1, nr):
        pl.semaphore_signal(
            barrier, inc=1, device_id=row_peer(o), device_id_type=pl.DeviceIdType.MESH
        )
    for o in range(1, nc):
        pl.semaphore_signal(
            barrier, inc=1, device_id=col_peer(o), device_id_type=pl.DeviceIdType.MESH
        )

    lane = iota((8, LANES), 1)
    lane_slot = lane % slots
    used = counts[0, 0]
    row_lane = jnp.full((8, LANES), -1, jnp.int32)
    col_lane = jnp.full((8, LANES), -1, jnp.int32)
    for k in range(slots):
        here = (lane_slot == k) & (k < used)
        row_lane = jnp.where(here, coords[0, 0, k, 0], row_lane)
        col_lane = jnp.where(here, coords[0, 0, k, 1], col_lane)
    row_ids[me_q] = row_lane.astype(F32)
    col_ids[me_p] = col_lane.astype(F32)

    pl.semaphore_wait(barrier, nr + nc - 2)

    sent = []

    def send_over_col(phase, source, target):
        copies = []
        for o in range(1, nc):
            copy = pltpu.make_async_remote_copy(
                src_ref=source(lax.rem(me_q + o, nc)),
                dst_ref=target.at[me_q],
                send_sem=send_col.at[phase, o - 1],
                recv_sem=recv_col.at[phase, o - 1],
                device_id=col_peer(o),
                device_id_type=pl.DeviceIdType.MESH,
            )
            copy.start()
            copies.append(copy)
        sent.extend(copies)
        return copies

    def send_over_row(phase, buffer):
        copies = []
        for o in range(1, nr):
            copy = pltpu.make_async_remote_copy(
                src_ref=buffer.at[me_p],
                dst_ref=buffer.at[me_p],
                send_sem=send_row.at[phase, o - 1],
                recv_sem=recv_row.at[phase, o - 1],
                device_id=row_peer(o),
                device_id_type=pl.DeviceIdType.MESH,
            )
            copy.start()
            copies.append(copy)
        sent.extend(copies)
        return copies

    def arrived(copies):
        for copy in copies:
            copy.wait_recv()

    row_ids_copies = send_over_col(0, lambda peer: row_ids.at[me_q], row_ids)
    col_ids_copies = send_over_row(0, col_ids)

    load_rhs.wait()
    squares = []
    for r in range(2):
        part = rhs_v[pl.ds(r, range_len, stride=2), :].astype(BF)
        ub[:, r * LANES : (r + 1) * LANES] = part
        values = part.astype(F32)
        line = jnp.sum(values * values, axis=0, keepdims=True)
        squares.append(jnp.sum(line, axis=1, keepdims=True))

    arrived(row_ids_copies)
    width = min(LANES, range_len)
    base = (me_q * range_len).astype(F32)
    for g in range(nc // per):
        ids = row_ids[g * per]
        for j in range(1, per):
            ids = jnp.where(lane // slots == j, row_ids[g * per + j], ids)
        local = jnp.broadcast_to(ids[0:1] - base, (LANES, LANES)).T[:, :width]
        column = iota((LANES, width), 1).astype(F32)
        onehot = jnp.concatenate(
            [
                jnp.where(local == column + float(c * width), 1.0, 0.0).astype(BF)
                for c in range(range_len // width)
            ],
            axis=1,
        )
        taken = jnp.dot(onehot, ub[...], preferred_element_type=F32).astype(BF)
        for j in range(per):
            for r in range(2):
                picks_out[g * per + j, r * slots : (r + 1) * slots, :] = taken[
                    j * slots : (j + 1) * slots, r * LANES : (r + 1) * LANES
                ]
    picks_copies = send_over_col(1, lambda peer: picks_out.at[peer], picks_in)
    picks_in[me_q] = picks_out[me_q]

    half_lane = lane // rows
    lane_r = ((lane // slots) % 2).astype(F32)

    def coded(first, second):
        return 2.0 * jnp.where(half_lane == 0, first, second) + lane_r

    def upright(code):
        return jnp.broadcast_to(code[0:1], (LANES, LANES)).T

    row_codes = [coded(row_ids[2 * s], row_ids[2 * s + 1]) for s in range(nc // 2)]
    for s in range(nc // 2):
        sub = upright(row_codes[s])
        sub_full[s * LANES : (s + 1) * LANES, :] = sub
        for t in range(nc // 2):
            code = row_codes[t][0:1]
            m_full[s * LANES : (s + 1) * LANES, t * LANES : (t + 1) * LANES] = jnp.where(
                (sub == code) & (code >= 0.0), 1.0, 0.0
            ).astype(BF)
    load_tiles.wait()
    block = tiles_v.shape[1]

    arrived(picks_copies)
    u0 = picks_in[0].astype(F32)
    for j in range(1, nc):
        u0 = u0 + picks_in[j].astype(F32)

    stacked = tiles_v[...].reshape(slots * block, block)
    c0_own = diagonal_dot(u0, stacked, slots).astype(BF)
    c0[me_p] = c0_own
    c0_copies = send_over_row(1, c0)

    arrived(col_ids_copies)
    sub_col = upright(coded(col_ids[me_p], col_ids[me_p]))[:rows]
    col_base = (me_p * (2 * range_len)).astype(F32)
    chunk = min(256, 2 * range_len)
    for s in range(nr // 2):
        code = coded(col_ids[2 * s], col_ids[2 * s + 1])[0:1]
        m_col[:, s * LANES : (s + 1) * LANES] = jnp.where(
            (sub_col == code) & (code >= 0.0), 1.0, 0.0
        ).astype(BF)
    for k in range(slots):
        tt[k * block : (k + 1) * block, :] = tiles_v[k].astype(F32).T.astype(BF)

    col_live = sub_col >= 0.0
    own_rows = pl.ds(pl.multiple_of(me_q * rows, rows), rows)
    m_row = m_full[own_rows, :]
    row_live = sub_full[own_rows, :] >= 0.0

    def total_col(buffer):
        return jnp.dot(
            m_col[...], buffer[...].reshape(nr * rows, LANES), preferred_element_type=F32
        )

    def total_row(matches, buffer):
        return jnp.dot(
            matches, buffer[...].reshape(nc * rows, LANES), preferred_element_type=F32
        )

    def inner(own, total, live):
        return per_realization(jnp.where(live, own.astype(F32) * total, 0.0), rows)

    arrived(c0_copies)
    g0 = total_col(c0)
    d0_own = diagonal_dot(g0, tt[...], slots).astype(BF)
    d0[me_q] = d0_own
    d0_copies = send_over_col(2, lambda peer: d0.at[me_q], d0)
    gg = inner(c0_own, g0, col_live)

    @pl.loop(0, 2 * range_len // chunk)
    def _(i):
        start = pl.multiple_of(i * chunk, chunk)
        row_number = iota((chunk, LANES), 0).astype(F32) + start.astype(F32)
        for s in range(nr // 2):
            code = coded(col_ids[2 * s], col_ids[2 * s + 1])[0:1]
            place[pl.ds(start, chunk), s * LANES : (s + 1) * LANES] = jnp.where(
                row_number == code - col_base, 1.0, 0.0
            ).astype(BF)

    arrived(d0_copies)
    f0 = total_row(m_row, d0)
    c1_own = diagonal_dot(f0, stacked, slots).astype(BF)
    c1[me_p] = c1_own
    c1_copies = send_over_row(2, c1)
    ff = inner(d0_own, f0, row_live)

    arrived(c1_copies)
    g1 = total_col(c1)
    d1_own = diagonal_dot(g1, tt[...], slots).astype(BF)
    d1[me_q] = d1_own
    d1_copies = send_over_col(3, lambda peer: d1.at[me_q], d1)
    hh = inner(c1_own, g1, col_live)

    stat_row = iota((16, LANES), 0)
    stats = jnp.zeros((16, LANES), F32)
    for s, pair in enumerate((squares, gg, ff, hh)):
        for r in range(2):
            stats = jnp.where(stat_row == 2 * s + r, pair[r], stats)
    stats_col[me_q] = stats
    stats_col_copies = send_over_col(4, lambda peer: stats_col.at[me_q], stats_col)

    arrived(d1_copies)
    f1 = total_row(m_full[...], d1)
    ee = per_realization(
        jnp.where(
            sub_full[...] >= 0.0, d1[...].reshape(nc * rows, LANES).astype(F32) * f1, 0.0
        ),
        rows,
    )
    arrived(stats_col_copies)
    group = jnp.sum(stats_col[...], axis=0)
    for r in range(2):
        group = jnp.where(stat_row == 8 + r, ee[r], group)
    stats_row[me_p] = group
    stats_row_copies = send_over_row(3, stats_row)
    arrived(stats_row_copies)
    whole = jnp.sum(stats_row[...], axis=0)

    uu, gg, ff, hh, ee = [whole[2 * s : 2 * s + 2] for s in range(5)]

    def norm(square):
        return jnp.sqrt(jnp.maximum(square, 0.0) + EPS)

    beta0 = norm(uu)
    alpha0 = norm(gg / (beta0 * beta0))
    a = 1.0 / (beta0 * alpha0)
    b = alpha0 / beta0
    beta1 = norm(a * a * ff - 2.0 * (a * b) * gg + b * b * uu)
    rho0 = jnp.sqrt(alpha0 * alpha0 + beta1 * beta1)
    cosine = alpha0 / rho0
    sine = beta1 / rho0
    phi0 = cosine * beta0
    phi_bar = sine * beta0
    x = a / beta1
    y = -(b / beta1 + beta1 * a)
    alpha1 = norm(x * x * hh + 2.0 * (x * y) * ff + y * y * gg)
    theta = sine * alpha1
    rho_bar = -cosine * alpha1
    e = x / alpha1
    h = y / alpha1 - (alpha1 / beta1) * a
    w = (alpha1 / beta1) * b
    beta2 = norm(
        e * e * ee + h * h * ff + w * w * uu
        + 2.0 * (e * h) * hh + 2.0 * (e * w) * ff + 2.0 * (h * w) * gg
    )
    rho1 = jnp.sqrt(rho_bar * rho_bar + beta2 * beta2)
    phi1 = (rho_bar / rho1) * phi_bar
    phi_ref[0:2, :] = (beta2 / rho1) * phi_bar
    on_g1 = (phi1 / rho1) * e
    on_g0 = (phi0 / rho0) * a + (phi1 / rho1) * (y / alpha1 - (theta / rho0) * a)

    first = iota((rows, LANES), 0) < slots
    scale0 = jnp.where(first, on_g0[0:1], on_g0[1:2])
    scale1 = jnp.where(first, on_g1[0:1], on_g1[1:2])
    terms = c0[...].astype(F32) * scale0[None] + c1[...].astype(F32) * scale1[None]
    terms = terms.reshape(nr * rows, LANES)
    high = terms.astype(BF)
    low = (terms - high.astype(F32)).astype(BF)
    both = jnp.concatenate([high, low], axis=1)

    @pl.loop(0, 2 * range_len // chunk)
    def _(i):
        here = pl.ds(pl.multiple_of(i * chunk, chunk), chunk)
        placed = jnp.dot(place[here, :], both, preferred_element_type=F32)
        out_ref[here, :] = placed[:, :LANES] + placed[:, LANES:]

    for copy in sent:
        copy.wait_send()


def on_device(nr, nc, tiles, coords, counts, rhs):
    slots, block = tiles.shape[2], tiles.shape[3]
    range_len = rhs.shape[1] // block
    rows = 2 * slots
    piece = rhs.reshape(2, range_len, block).transpose(1, 0, 2).reshape(2 * range_len, block)
    dma = pltpu.SemaphoreType.DMA
    placed, phi = pl.pallas_call(
        functools.partial(solver, nr, nc, slots, range_len),
        out_shape=(
            jax.ShapeDtypeStruct((2 * range_len, block), F32),
            jax.ShapeDtypeStruct((8, LANES), F32),
        ),
        in_specs=[
            pl.BlockSpec(memory_space=pltpu.SMEM),
            pl.BlockSpec(memory_space=pltpu.SMEM),
            pl.BlockSpec(memory_space=pl.ANY),
            pl.BlockSpec(memory_space=pl.ANY),
        ],
        out_specs=(
            pl.BlockSpec(memory_space=pltpu.VMEM),
            pl.BlockSpec(memory_space=pltpu.VMEM),
        ),
        scratch_shapes=[
            pltpu.VMEM((2 * range_len, block), F32),
            pltpu.VMEM((range_len, 2 * block), BF),
            pltpu.VMEM((slots, block, block), BF),
            pltpu.VMEM((slots * block, block), BF),
            pltpu.VMEM((nc, 8, LANES), F32),
            pltpu.VMEM((nr, 8, LANES), F32),
            pltpu.VMEM((nc, rows, block), BF),
            pltpu.VMEM((nc, rows, block), BF),
            pltpu.VMEM((nr, rows, block), BF),
            pltpu.VMEM((nr, rows, block), BF),
            pltpu.VMEM((nc, rows, block), BF),
            pltpu.VMEM((nc, rows, block), BF),
            pltpu.VMEM((nc, 16, LANES), F32),
            pltpu.VMEM((nr, 16, LANES), F32),
            pltpu.VMEM((rows, nr * rows), BF),
            pltpu.VMEM((nc * rows, nc * rows), BF),
            pltpu.VMEM((nc * rows, LANES), F32),
            pltpu.VMEM((2 * range_len, nr * rows), BF),
            dma((2,)),
            dma((5, nc - 1)),
            dma((5, nc - 1)),
            dma((4, nr - 1)),
            dma((4, nr - 1)),
        ],
        compiler_params=pltpu.CompilerParams(
            collective_id=0, has_side_effects=True, vmem_limit_bytes=48 * 1024 * 1024
        ),
    )(coords, counts, tiles[0, 0], piece)
    answer = placed.reshape(range_len, 2, block).transpose(1, 0, 2).reshape(2, range_len * block)
    return answer, phi[:2, 0]


def solution(mesh):
    nr, nc = mesh.shape["row"], mesh.shape["col"]
    return jax.shard_map(
        functools.partial(on_device, nr, nc),
        mesh=mesh,
        in_specs=(
            P("row", "col", None, None, None),
            P("row", "col", None, None),
            P("row", "col"),
            P(None, ("row", "col")),
        ),
        out_specs=(P(None, ("col", "row")), P()),
        check_vma=False,
    )
```

time: 991 us -> 42.8 us (0.04); the launches traced: 981 us -> 42.6 us
  local copies, waits for them, and re-layouts: 628 us -> 4.8 us
  blocking collectives: 197 us -> 0 us
  waiting for transfers between devices: 72.7 us -> 0 us
  Pallas kernels: 0 us -> 36.5 us
  other arithmetic: 35.4 us -> 0 us
  starting transfers between devices: 28.2 us -> 0 us
  between operations: 14.6 us -> 1.3 us
    gather x4 -> x0, local copies, waits for them, and re-layouts: 460 us -> none  [select_blocks(): jnp.take(piece, clipped.reshape(-1), axis=1)]
    psum x5 -> x0, blocking collectives: 197 us -> none  [own_norm(): lax.psum(jnp.sum(values * values, axis=1), ('row', 'col')) + EPS]
    all_gather x2 -> x0, local copies, waits for them, and re-layouts: 157 us -> none  [gather_u(): return fold_rows(lax.all_gather(u_rounded, 'col', axis=1, tiled=True))]
    all_gather x4 -> x0, waiting for transfers between devices: 50.3 us -> none  [the longest x2 50.3 us: gather_v(): return fold_cols(lax.all_gather(v_rounded, 'row', axis=1, tiled=True))]
    pallas_call x0 -> x1, Pallas kernels: none -> 36.5 us  [on_device(): pl.pallas_call(functools.partial(solver, nr, nc, slots, range_len), out_s...]
    all_to_all x6 -> x0, starting transfers between devices: 27.8 us -> none  [the longest x2 10.6 us: adjoint(): lax.all_to_all(sent, 'row', split_axis=0, concat_axis=0, tiled=True)]
    all_to_all x6 -> x0, waiting for transfers between devices: 22.3 us -> none  [the longest x2 11.8 us: adjoint(): lax.all_to_all(sent, 'row', split_axis=0, concat_axis=0, tiled=True)]
    convert_element_type x6 -> x0, other arithmetic: 12.9 us -> none  [the longest x5 12.9 us: rounded(): return lax.optimization_barrier(values.astype(jnp.bfloat16))]
  transfers between devices with their start and end apart: 10 -> 0, of which waited for: 7 -> 0; matrix products, arithmetic and copies ran while one was open for 14% -> 0% of each run, Pallas kernels for 0% -> 0%
where the time goes in v1:
time: 42.8 us; the launch traced here: 42.6 us
  Pallas kernels  36.5 us (85%)
  local copies, waits for them, and re-layouts  4.8 us (11%)
  between operations  1.3 us (3%)
    pallas_call x1, Pallas kernels, on_device(): pl.pallas_call(functools.partial(solver, nr, nc, slots, range_len), out_s...  36.5 us
    unnamed x8, local copies, waits for them, and re-layouts  4.18 us

profile of v1, /device:TPU:0, one launch (start us, length us, event | category | flops | bytes accessed | tf_op | source)
XLA Modules:
  0.0 42.6 jit_solution(16389050409010011476)
XLA Ops:
  1.3 0.0 copy-start.2
  1.3 0.7 %copy-done.2 = s32[1,1,32,2]{2,3,1,0:T(2,128)S(1)} copy-done((s32[1,1,32,2]{2,3,1,0:T(2,128)S(1)}, s32[1,1,32,2]{2,3,1,0:T(2,128)}, u32[]{:S(2)}) %copy-start.2) | copy-done | bytes 280
  2.0 0.1 copy.10.coords
  2.0 0.0 copy-start
  2.0 1.2 %copy-done = bf16[1,1,32,128,128]{4,3,2,1,0:T(8,128)(2,1)S(1)} copy-done((bf16[1,1,32,128,128]{4,3,2,1,0:T(8,128)(2,1)S(1)}, bf16[1,1,32,128,128]{4,3,2,1,0:T(8,128)(2,1)}, u32[]{:S(2)}) %copy-start) | copy-done | bytes 1048600
  3.3 0.0 copy-start.1
  3.3 1.2 %copy-done.1 = f32[2,131072]{1,0:T(2,128)S(1)} copy-done((f32[2,131072]{1,0:T(2,128)S(1)}, f32[2,131072]{1,0:T(2,128)}, u32[]{:S(2)}) %copy-start.1) | copy-done | bytes 1048600
  4.5 36.5 %shard_map.59 = (f32[2048,128]{1,0:T(8,128)S(1)}, f32[8,128]{1,0:T(8,128)S(1)}) custom-call(s32[1,1,32,2]{3,2,1,0:T(8,128)S(1)} %copy.10.coords, s32[1,1]{1,0:T(1,128)S(6)} %copy.13.counts, bf16[32,128,128]{2,1,0:T(8,128)(2,1)S(1)} %bitcast.11, f32[2048,128]{1,0:T(8,128)S(1)} %bitcast.12), custom_call_target="tpu_custom_call" | custom-call | tf_op jit(solution)/shard_map/pallas_call | solution.py:333
  41.0 0.6 %slice_reduce_fusion = f32[2]{0:T(128)} fusion(f32[8,128]{1,0:T(8,128)S(1)} %get-tuple-element.5), kind=kLoop, calls=%fused_computation | loop fusion | bytes 16 | tf_op jit(solution)/shard_map/slice | solution.py:379
  41.6 1.0 %copy.14 = f32[2,131072]{1,0:T(2,128)} copy(f32[2,131072]{1,0:T(2,128)S(1)} %bitcast.13) | data formatting | bytes 2097152
Async XLA Ops:
  1.3 0.7 %copy-start.2 = (s32[1,1,32,2]{2,3,1,0:T(2,128)S(1)}, s32[1,1,32,2]{2,3,1,0:T(2,128)}, u32[]{:S(2)}) copy-start(s32[1,1,32,2]{2,3,1,0:T(2,128)} %param.5) | copy-start | bytes 772
  2.0 1.2 %copy-start = (bf16[1,1,32,128,128]{4,3,2,1,0:T(8,128)(2,1)S(1)}, bf16[1,1,32,128,128]{4,3,2,1,0:T(8,128)(2,1)}, u32[]{:S(2)}) copy-start(bf16[1,1,32,128,128]{4,3,2,1,0:T(8,128)(2,1)} %param.4) | copy-start | bytes 3145732
  3.3 1.2 %copy-start.1 = (f32[2,131072]{1,0:T(2,128)S(1)}, f32[2,131072]{1,0:T(2,128)}, u32[]{:S(2)}) copy-start(f32[2,131072]{1,0:T(2,128)} %param.7) | copy-start | bytes 3145732

commit v2 on v1

--- a/solution.py
+++ b/solution.py
@@ -18,11 +18,24 @@
 
 
 def diagonal_dot(values, stacked, slots):
-    row_slot = iota(values.shape, 0) % slots
-    wide = jnp.concatenate(
-        [jnp.where(row_slot == k, values, 0.0).astype(BF) for k in range(slots)], axis=1
-    )
-    return jnp.dot(wide, stacked, preferred_element_type=F32)
+    group = 8
+    row_slot = iota((2 * group, LANES), 0) % group
+    parts = []
+    for start in range(0, slots, group):
+        pair = jnp.concatenate(
+            [values[r * slots + start : r * slots + start + group] for r in range(2)], axis=0
+        )
+        wide = jnp.concatenate(
+            [jnp.where(row_slot == k, pair, 0.0).astype(BF) for k in range(group)], axis=1
+        )
+        parts.append(
+            jnp.dot(
+                wide,
+                stacked[start * LANES : (start + group) * LANES],
+                preferred_element_type=F32,
+            )
+        )
+    return jnp.concatenate([p[:group] for p in parts] + [p[group:] for p in parts], axis=0)
 
 
 def per_realization(products, rows):
@@ -34,10 +47,10 @@
 
 def solver(
     nr, nc, slots, range_len,
-    coords, counts, tiles_hbm, rhs_hbm,
+    coords_hbm, counts, tiles_hbm, rhs_hbm,
     out_ref, phi_ref,
-    rhs_v, ub, tiles_v, tt, row_ids, col_ids, picks_out, picks_in, c0, c1, d0, d1,
-    stats_col, stats_row, m_col, m_full, sub_full, place,
+    coords_v, rhs_v, ub, tiles_v, tt, row_ids, col_ids, picks_out, picks_in, c0, c1, d0, d1,
+    stats_col, stats_row, m_col, m_full, sub_full, place, placed1,
     load_sem, send_col, recv_col, send_row, recv_row,
 ):
     me_p = lax.axis_index("row")
@@ -47,6 +60,8 @@
 
     load_rhs = pltpu.make_async_copy(rhs_hbm, rhs_v, load_sem.at[0])
     load_tiles = pltpu.make_async_copy(tiles_hbm, tiles_v, load_sem.at[1])
+    load_coords = pltpu.make_async_copy(coords_hbm, coords_v, load_sem.at[2])
+    load_coords.start()
     load_rhs.start()
     load_tiles.start()
 
@@ -66,17 +81,12 @@
             barrier, inc=1, device_id=col_peer(o), device_id_type=pl.DeviceIdType.MESH
         )
 
-    lane = iota((8, LANES), 1)
-    lane_slot = lane % slots
-    used = counts[0, 0]
-    row_lane = jnp.full((8, LANES), -1, jnp.int32)
-    col_lane = jnp.full((8, LANES), -1, jnp.int32)
-    for k in range(slots):
-        here = (lane_slot == k) & (k < used)
-        row_lane = jnp.where(here, coords[0, 0, k, 0], row_lane)
-        col_lane = jnp.where(here, coords[0, 0, k, 1], col_lane)
-    row_ids[me_q] = row_lane.astype(F32)
-    col_ids[me_p] = col_lane.astype(F32)
+    lane = iota((1, LANES), 1)
+    load_coords.wait()
+    numbers = jnp.concatenate([coords_v[...]] * per, axis=1)
+    numbers = jnp.where(iota((2, LANES), 1) % slots < counts[0, 0], numbers, -1).astype(F32)
+    row_ids[me_q] = numbers[0:1]
+    col_ids[me_p] = numbers[1:2]
 
     pl.semaphore_wait(barrier, nr + nc - 2)
 
@@ -137,7 +147,7 @@
         ids = row_ids[g * per]
         for j in range(1, per):
             ids = jnp.where(lane // slots == j, row_ids[g * per + j], ids)
-        local = jnp.broadcast_to(ids[0:1] - base, (LANES, LANES)).T[:, :width]
+        local = jnp.broadcast_to(ids - base, (LANES, LANES)).T[:, :width]
         column = iota((LANES, width), 1).astype(F32)
         onehot = jnp.concatenate(
             [
@@ -162,20 +172,26 @@
         return 2.0 * jnp.where(half_lane == 0, first, second) + lane_r
 
     def upright(code):
-        return jnp.broadcast_to(code[0:1], (LANES, LANES)).T
+        return jnp.broadcast_to(code, (LANES, LANES)).T
 
     row_codes = [coded(row_ids[2 * s], row_ids[2 * s + 1]) for s in range(nc // 2)]
     for s in range(nc // 2):
         sub = upright(row_codes[s])
         sub_full[s * LANES : (s + 1) * LANES, :] = sub
         for t in range(nc // 2):
-            code = row_codes[t][0:1]
+            code = row_codes[t]
             m_full[s * LANES : (s + 1) * LANES, t * LANES : (t + 1) * LANES] = jnp.where(
                 (sub == code) & (code >= 0.0), 1.0, 0.0
             ).astype(BF)
     load_tiles.wait()
     block = tiles_v.shape[1]
 
+    def turn(first, last):
+        for k in range(first, last):
+            tt[k * block : (k + 1) * block, :] = tiles_v[k].astype(F32).T.astype(BF)
+
+    turn(0, slots // 2)
+
     arrived(picks_copies)
     u0 = picks_in[0].astype(F32)
     for j in range(1, nc):
@@ -191,12 +207,11 @@
     col_base = (me_p * (2 * range_len)).astype(F32)
     chunk = min(256, 2 * range_len)
     for s in range(nr // 2):
-        code = coded(col_ids[2 * s], col_ids[2 * s + 1])[0:1]
+        code = coded(col_ids[2 * s], col_ids[2 * s + 1])
         m_col[:, s * LANES : (s + 1) * LANES] = jnp.where(
             (sub_col == code) & (code >= 0.0), 1.0, 0.0
         ).astype(BF)
-    for k in range(slots):
-        tt[k * block : (k + 1) * block, :] = tiles_v[k].astype(F32).T.astype(BF)
+    turn(slots // 2, slots)
 
     col_live = sub_col >= 0.0
     own_rows = pl.ds(pl.multiple_of(me_q * rows, rows), rows)
@@ -215,6 +230,16 @@
 
     def inner(own, total, live):
         return per_realization(jnp.where(live, own.astype(F32) * total, 0.0), rows)
+
+    @pl.loop(0, 2 * range_len // chunk)
+    def _(i):
+        start = pl.multiple_of(i * chunk, chunk)
+        row_number = iota((chunk, LANES), 0).astype(F32) + start.astype(F32)
+        for s in range(nr // 2):
+            code = coded(col_ids[2 * s], col_ids[2 * s + 1])
+            place[pl.ds(start, chunk), s * LANES : (s + 1) * LANES] = jnp.where(
+                row_number == code - col_base, 1.0, 0.0
+            ).astype(BF)
 
     arrived(c0_copies)
     g0 = total_col(c0)
@@ -223,16 +248,6 @@
     d0_copies = send_over_col(2, lambda peer: d0.at[me_q], d0)
     gg = inner(c0_own, g0, col_live)
 
-    @pl.loop(0, 2 * range_len // chunk)
-    def _(i):
-        start = pl.multiple_of(i * chunk, chunk)
-        row_number = iota((chunk, LANES), 0).astype(F32) + start.astype(F32)
-        for s in range(nr // 2):
-            code = coded(col_ids[2 * s], col_ids[2 * s + 1])[0:1]
-            place[pl.ds(start, chunk), s * LANES : (s + 1) * LANES] = jnp.where(
-                row_number == code - col_base, 1.0, 0.0
-            ).astype(BF)
-
     arrived(d0_copies)
     f0 = total_row(m_row, d0)
     c1_own = diagonal_dot(f0, stacked, slots).astype(BF)
@@ -240,6 +255,15 @@
     c1_copies = send_over_row(2, c1)
     ff = inner(d0_own, f0, row_live)
 
+    def put(buffer, target):
+        flat = buffer[...].reshape(nr * rows, LANES)
+
+        @pl.loop(0, 2 * range_len // chunk)
+        def _(i):
+            here = pl.ds(pl.multiple_of(i * chunk, chunk), chunk)
+            target[here, :] = jnp.dot(place[here, :], flat, preferred_element_type=F32)
+
+    put(c0, out_ref)
     arrived(c1_copies)
     g1 = total_col(c1)
     d1_own = diagonal_dot(g1, tt[...], slots).astype(BF)
@@ -247,14 +271,14 @@
     d1_copies = send_over_col(3, lambda peer: d1.at[me_q], d1)
     hh = inner(c1_own, g1, col_live)
 
-    stat_row = iota((16, LANES), 0)
-    stats = jnp.zeros((16, LANES), F32)
+    stats = jnp.zeros((1, LANES), F32)
     for s, pair in enumerate((squares, gg, ff, hh)):
         for r in range(2):
-            stats = jnp.where(stat_row == 2 * s + r, pair[r], stats)
+            stats = jnp.where(lane == 2 * s + r, pair[r], stats)
     stats_col[me_q] = stats
     stats_col_copies = send_over_col(4, lambda peer: stats_col.at[me_q], stats_col)
 
+    put(c1, placed1)
     arrived(d1_copies)
     f1 = total_row(m_full[...], d1)
     ee = per_realization(
@@ -266,13 +290,13 @@
     arrived(stats_col_copies)
     group = jnp.sum(stats_col[...], axis=0)
     for r in range(2):
-        group = jnp.where(stat_row == 8 + r, ee[r], group)
+        group = jnp.where(lane == 8 + r, ee[r], group)
     stats_row[me_p] = group
     stats_row_copies = send_over_row(3, stats_row)
     arrived(stats_row_copies)
     whole = jnp.sum(stats_row[...], axis=0)
 
-    uu, gg, ff, hh, ee = [whole[2 * s : 2 * s + 2] for s in range(5)]
+    uu, gg, ff, hh, ee = [whole] + [pltpu.roll(whole, LANES - 2 * s, 1) for s in range(1, 5)]
 
     def norm(square):
         return jnp.sqrt(jnp.maximum(square, 0.0) + EPS)
@@ -301,24 +325,18 @@
     )
     rho1 = jnp.sqrt(rho_bar * rho_bar + beta2 * beta2)
     phi1 = (rho_bar / rho1) * phi_bar
-    phi_ref[0:2, :] = (beta2 / rho1) * phi_bar
+    phi_ref[...] = ((beta2 / rho1) * phi_bar)[:, 0:2]
     on_g1 = (phi1 / rho1) * e
     on_g0 = (phi0 / rho0) * a + (phi1 / rho1) * (y / alpha1 - (theta / rho0) * a)
 
-    first = iota((rows, LANES), 0) < slots
-    scale0 = jnp.where(first, on_g0[0:1], on_g0[1:2])
-    scale1 = jnp.where(first, on_g1[0:1], on_g1[1:2])
-    terms = c0[...].astype(F32) * scale0[None] + c1[...].astype(F32) * scale1[None]
-    terms = terms.reshape(nr * rows, LANES)
-    high = terms.astype(BF)
-    low = (terms - high.astype(F32)).astype(BF)
-    both = jnp.concatenate([high, low], axis=1)
+    even = iota((chunk, LANES), 0) % 2 == 0
+    scale0 = jnp.where(even, on_g0[:, 0:1], on_g0[:, 1:2])
+    scale1 = jnp.where(even, on_g1[:, 0:1], on_g1[:, 1:2])
 
     @pl.loop(0, 2 * range_len // chunk)
     def _(i):
         here = pl.ds(pl.multiple_of(i * chunk, chunk), chunk)
-        placed = jnp.dot(place[here, :], both, preferred_element_type=F32)
-        out_ref[here, :] = placed[:, :LANES] + placed[:, LANES:]
+        out_ref[here, :] = out_ref[here, :] * scale0 + placed1[here, :] * scale1
 
     for copy in sent:
         copy.wait_send()
@@ -334,38 +352,40 @@
         functools.partial(solver, nr, nc, slots, range_len),
         out_shape=(
             jax.ShapeDtypeStruct((2 * range_len, block), F32),
-            jax.ShapeDtypeStruct((8, LANES), F32),
+            jax.ShapeDtypeStruct((1, 2), F32),
         ),
         in_specs=[
+            pl.BlockSpec(memory_space=pltpu.HBM),
             pl.BlockSpec(memory_space=pltpu.SMEM),
-            pl.BlockSpec(memory_space=pltpu.SMEM),
-            pl.BlockSpec(memory_space=pl.ANY),
-            pl.BlockSpec(memory_space=pl.ANY),
+            pl.BlockSpec(memory_space=pltpu.HBM),
+            pl.BlockSpec(memory_space=pltpu.HBM),
         ],
         out_specs=(
             pl.BlockSpec(memory_space=pltpu.VMEM),
             pl.BlockSpec(memory_space=pltpu.VMEM),
         ),
         scratch_shapes=[
+            pltpu.VMEM((2, slots), jnp.int32),
             pltpu.VMEM((2 * range_len, block), F32),
             pltpu.VMEM((range_len, 2 * block), BF),
             pltpu.VMEM((slots, block, block), BF),
             pltpu.VMEM((slots * block, block), BF),
-            pltpu.VMEM((nc, 8, LANES), F32),
-            pltpu.VMEM((nr, 8, LANES), F32),
+            pltpu.VMEM((nc, 1, LANES), F32),
+            pltpu.VMEM((nr, 1, LANES), F32),
             pltpu.VMEM((nc, rows, block), BF),
             pltpu.VMEM((nc, rows, block), BF),
             pltpu.VMEM((nr, rows, block), BF),
             pltpu.VMEM((nr, rows, block), BF),
             pltpu.VMEM((nc, rows, block), BF),
             pltpu.VMEM((nc, rows, block), BF),
-            pltpu.VMEM((nc, 16, LANES), F32),
-            pltpu.VMEM((nr, 16, LANES), F32),
+            pltpu.VMEM((nc, 1, LANES), F32),
+            pltpu.VMEM((nr, 1, LANES), F32),
             pltpu.VMEM((rows, nr * rows), BF),
             pltpu.VMEM((nc * rows, nc * rows), BF),
             pltpu.VMEM((nc * rows, LANES), F32),
             pltpu.VMEM((2 * range_len, nr * rows), BF),
-            dma((2,)),
+            pltpu.VMEM((2 * range_len, block), F32),
+            dma((3,)),
             dma((5, nc - 1)),
             dma((5, nc - 1)),
             dma((4, nr - 1)),
@@ -374,9 +394,9 @@
         compiler_params=pltpu.CompilerParams(
             collective_id=0, has_side_effects=True, vmem_limit_bytes=48 * 1024 * 1024
         ),
-    )(coords, counts, tiles[0, 0], piece)
+    )(coords[0, 0].T, counts, tiles[0, 0], piece)
     answer = placed.reshape(range_len, 2, block).transpose(1, 0, 2).reshape(2, range_len * block)
-    return answer, phi[:2, 0]
+    return answer, phi[0]
 
 
 def solution(mesh):

time: 42.8 us -> 39.9 us (0.932)
  Pallas kernels: 36.5 us -> 33.8 us
    pallas_call x1, Pallas kernels: 36.5 us -> 33.8 us  [on_device(): pl.pallas_call(functools.partial(solver, nr, nc, slots, range_len), out_s...]
    slice x1 -> x0, local copies, waits for them, and re-layouts: 0.63 us -> none  [on_device(): return (answer, phi[:2, 0])]
where the time goes in v2:
time: 39.9 us; the launch traced here: 39.7 us
  Pallas kernels  33.8 us (85%)
  local copies, waits for them, and re-layouts  4.6 us (12%)
  between operations  1.3 us (3%)
    pallas_call x1, Pallas kernels, on_device(): pl.pallas_call(functools.partial(solver, nr, nc, slots, range_len), out_s...  33.8 us
    unnamed x8, local copies, waits for them, and re-layouts  4.6 us

profile of v2, /device:TPU:0, one launch (start us, length us, event | category | flops | bytes accessed | tf_op | source)
XLA Modules:
  0.0 39.7 jit_solution(5909625741511561156)
XLA Ops:
  1.3 0.0 copy-start.2
  1.3 0.7 %copy-done.2 = s32[1,1,32,2]{2,3,1,0:T(2,128)S(1)} copy-done((s32[1,1,32,2]{2,3,1,0:T(2,128)S(1)}, s32[1,1,32,2]{2,3,1,0:T(2,128)}, u32[]{:S(2)}) %copy-start.2) | copy-done | bytes 280
  2.0 0.0 copy-start
  2.0 1.2 %copy-done = bf16[1,1,32,128,128]{4,3,2,1,0:T(8,128)(2,1)S(1)} copy-done((bf16[1,1,32,128,128]{4,3,2,1,0:T(8,128)(2,1)S(1)}, bf16[1,1,32,128,128]{4,3,2,1,0:T(8,128)(2,1)}, u32[]{:S(2)}) %copy-start) | copy-done | bytes 1048600
  3.2 0.0 copy-start.1
  3.2 1.2 %copy-done.1 = f32[2,131072]{1,0:T(2,128)S(1)} copy-done((f32[2,131072]{1,0:T(2,128)S(1)}, f32[2,131072]{1,0:T(2,128)}, u32[]{:S(2)}) %copy-start.1) | copy-done | bytes 1048600
  4.4 33.8 %shard_map.59 = (f32[2048,128]{1,0:T(8,128)S(1)}, f32[1,2]{1,0:T(1,128)S(1)}) custom-call(s32[2,32]{1,0:T(2,128)S(1)} %bitcast.18, s32[1,1]{1,0:T(1,128)S(6)} %copy.10.counts, bf16[32,128,128]{2,1,0:T(8,128)(2,1)S(1)} %bitcast.15, f32[2048,128]{1,0:T(8,128)S(1)} %bitcast.16), custom_call_target="tpu_custom_call" | custom-call | tf_op jit(solution)/shard_map/pallas_call | solution.py:351
  38.2 1.0 %copy.11 = f32[2,131072]{1,0:T(2,128)} copy(f32[2,131072]{1,0:T(2,128)S(1)} %bitcast.17) | data formatting | bytes 2097152
  39.2 0.5 %copy.12 = f32[2]{0:T(128)} copy(f32[2]{0:T(128)S(1)} %bitcast.19) | data formatting | bytes 16
Async XLA Ops:
  1.3 0.7 %copy-start.2 = (s32[1,1,32,2]{2,3,1,0:T(2,128)S(1)}, s32[1,1,32,2]{2,3,1,0:T(2,128)}, u32[]{:S(2)}) copy-start(s32[1,1,32,2]{2,3,1,0:T(2,128)} %param.5) | copy-start | bytes 772
  2.0 1.2 %copy-start = (bf16[1,1,32,128,128]{4,3,2,1,0:T(8,128)(2,1)S(1)}, bf16[1,1,32,128,128]{4,3,2,1,0:T(8,128)(2,1)}, u32[]{:S(2)}) copy-start(bf16[1,1,32,128,128]{4,3,2,1,0:T(8,128)(2,1)} %param.4) | copy-start | bytes 3145732
  3.2 1.2 %copy-start.1 = (f32[2,131072]{1,0:T(2,128)S(1)}, f32[2,131072]{1,0:T(2,128)}, u32[]{:S(2)}) copy-start(f32[2,131072]{1,0:T(2,128)} %param.7) | copy-start | bytes 3145732

commit v3 on v2

--- a/solution.py
+++ b/solution.py
@@ -278,7 +278,6 @@
     stats_col[me_q] = stats
     stats_col_copies = send_over_col(4, lambda peer: stats_col.at[me_q], stats_col)
 
-    put(c1, placed1)
     arrived(d1_copies)
     f1 = total_row(m_full[...], d1)
     ee = per_realization(
@@ -293,6 +292,7 @@
         group = jnp.where(lane == 8 + r, ee[r], group)
     stats_row[me_p] = group
     stats_row_copies = send_over_row(3, stats_row)
+    put(c1, placed1)
     arrived(stats_row_copies)
     whole = jnp.sum(stats_row[...], axis=0)
 
@@ -394,7 +394,12 @@
         compiler_params=pltpu.CompilerParams(
             collective_id=0, has_side_effects=True, vmem_limit_bytes=48 * 1024 * 1024
         ),
-    )(coords[0, 0].T, counts, tiles[0, 0], piece)
+    )(
+        pltpu.with_memory_space_constraint(coords[0, 0].T, pltpu.HBM),
+        counts,
+        pltpu.with_memory_space_constraint(tiles[0, 0], pltpu.HBM),
+        pltpu.with_memory_space_constraint(piece, pltpu.HBM),
+    )
     answer = placed.reshape(range_len, 2, block).transpose(1, 0, 2).reshape(2, range_len * block)
     return answer, phi[0]
 

time: 39.9 us -> 36.6 us (0.917)
  local copies, waits for them, and re-layouts: 4.6 us -> 1.48 us
    unnamed x8 -> x2, local copies, waits for them, and re-layouts: 4.6 us -> 1.48 us
where the time goes in v3:
time: 36.6 us; the launch traced here: 36.4 us
  Pallas kernels  33.7 us (92%)
  local copies, waits for them, and re-layouts  1.48 us (4%)
  between operations  1.28 us (3%)
    pallas_call x1, Pallas kernels, on_device(): pl.pallas_call(functools.partial(solver, nr, nc, slots, range_len), out_s...  33.7 us
    unnamed x2, local copies, waits for them, and re-layouts  1.48 us

profile of v3, /device:TPU:0, one launch (start us, length us, event | category | flops | bytes accessed | tf_op | source)
XLA Modules:
  0.0 36.4 jit_solution(14827096596631053730)
XLA Ops:
  1.3 33.7 %shard_map.59 = (f32[2048,128]{1,0:T(8,128)S(1)}, f32[1,2]{1,0:T(1,128)S(1)}) custom-call(s32[2,32]{1,0:T(2,128)} %bitcast.19, s32[1,1]{1,0:T(1,128)S(6)} %copy.10.counts, bf16[32,128,128]{2,1,0:T(8,128)(2,1)} %bitcast.17, f32[2048,128]{1,0:T(8,128)} %bitcast.18), custom_call_target="tpu_custom_call" | custom-call | tf_op jit(solution)/shard_map/pallas_call | solution.py:351
  34.9 1.0 %copy.11 = f32[2,131072]{1,0:T(2,128)} copy(f32[2,131072]{1,0:T(2,128)S(1)} %bitcast.15) | data formatting | bytes 2097152
  35.9 0.5 %copy.12 = f32[2]{0:T(128)} copy(f32[2]{0:T(128)S(1)} %bitcast.16) | data formatting | bytes 16

commit v4 on v3

v4 whole, which is shorter than its diff:
```python
import functools

import jax
import jax.numpy as jnp
from jax import lax
from jax.experimental import pallas as pl
from jax.experimental.pallas import tpu as pltpu
from jax.sharding import PartitionSpec as P

EPS = 1e-06
LANES = 128
BF = jnp.bfloat16
F32 = jnp.float32


def iota(shape, dim):
    return lax.broadcasted_iota(jnp.int32, shape, dim)


def diagonal_dot(values, stacked, slots):
    group, half = 8, slots // 2
    row_slot = iota((2 * group, LANES), 0) % group
    first, second = [], []
    for start in range(0, half, group):
        pair = jnp.concatenate(
            [values[start : start + group], values[half + start : half + start + group]], axis=0
        )
        wide = jnp.concatenate(
            [jnp.where(row_slot == k, pair, 0.0).astype(BF) for k in range(group)], axis=1
        )
        result = jnp.dot(
            wide,
            stacked[start * LANES : (start + group) * LANES],
            preferred_element_type=F32,
        )
        first.append(result[:group, :LANES])
        second.append(result[group:, LANES:])
    return jnp.concatenate(first + second, axis=0)


def total_of(products):
    line = jnp.sum(products, axis=0, keepdims=True)
    return jnp.sum(line, axis=1, keepdims=True)


def solver(
    nr, nc, slots, range_len,
    coords_hbm, counts, tiles_hbm, rhs_hbm,
    out_ref, phi_ref,
    coords_v, rhs_v, ub, tiles_v, tt, row_ids, col_ids, picks_out, picks_in, c0, c1, d0, d1,
    stats_col, stats_row, m_col, m_full, sub_full, place, placed0, placed1,
    load_sem, send_col, recv_col, send_row, recv_row,
):
    me_p = lax.axis_index("row")
    me_q = lax.axis_index("col")
    per = LANES // slots

    load_rhs = pltpu.make_async_copy(rhs_hbm, rhs_v, load_sem.at[0])
    half = slots // 2
    load_tiles = [
        pltpu.make_async_copy(
            tiles_hbm.at[i * half : (i + 1) * half],
            tiles_v.at[:, :, i * LANES : (i + 1) * LANES],
            load_sem.at[1 + i],
        )
        for i in range(2)
    ]
    load_coords = pltpu.make_async_copy(coords_hbm, coords_v, load_sem.at[3])
    load_coords.start()
    load_rhs.start()
    for load in load_tiles:
        load.start()

    def row_peer(o):
        return (lax.rem(me_p + o, nr), me_q)

    def col_peer(o):
        return (me_p, lax.rem(me_q + o, nc))

    barrier = pltpu.get_barrier_semaphore()
    for o in range(1, nr):
        pl.semaphore_signal(
            barrier, inc=1, device_id=row_peer(o), device_id_type=pl.DeviceIdType.MESH
        )
    for o in range(1, nc):
        pl.semaphore_signal(
            barrier, inc=1, device_id=col_peer(o), device_id_type=pl.DeviceIdType.MESH
        )

    lane = iota((1, LANES), 1)
    load_coords.wait()
    numbers = jnp.concatenate([coords_v[...]] * per, axis=1)
    numbers = jnp.where(iota((2, LANES), 1) % slots < counts[0, 0], numbers, -1).astype(F32)
    row_ids[me_q] = numbers[0:1]
    col_ids[me_p] = numbers[1:2]

    pl.semaphore_wait(barrier, nr + nc - 2)

    sent = []

    def send_over_col(phase, source, mine):
        copies = []
        for o in range(1, nc):
            copy = pltpu.make_async_remote_copy(
                src_ref=source(lax.rem(me_q + o, nc)),
                dst_ref=mine,
                send_sem=send_col.at[phase, o - 1],
                recv_sem=recv_col.at[phase, o - 1],
                device_id=col_peer(o),
                device_id_type=pl.DeviceIdType.MESH,
            )
            copy.start()
            copies.append(copy)
        sent.extend(copies)
        return copies

    def send_over_row(phase, mine):
        copies = []
        for o in range(1, nr):
            copy = pltpu.make_async_remote_copy(
                src_ref=mine,
                dst_ref=mine,
                send_sem=send_row.at[phase, o - 1],
                recv_sem=recv_row.at[phase, o - 1],
                device_id=row_peer(o),
                device_id_type=pl.DeviceIdType.MESH,
            )
            copy.start()
            copies.append(copy)
        sent.extend(copies)
        return copies

    def arrived(copies):
        for copy in copies:
            copy.wait_recv()

    row_ids_copies = send_over_col(0, lambda peer: row_ids.at[me_q], row_ids.at[me_q])
    col_ids_copies = send_over_row(0, col_ids.at[me_p])

    load_rhs.wait()
    squares = []
    for r in range(2):
        part = rhs_v[pl.ds(r, range_len, stride=2), :].astype(BF)
        ub[:, r * LANES : (r + 1) * LANES] = part
        values = part.astype(F32)
        squares.append(total_of(values * values))

    arrived(row_ids_copies)

    def joined(ids_ref, g):
        ids = ids_ref[g * per]
        for j in range(1, per):
            ids = jnp.where(lane // slots == j, ids_ref[g * per + j], ids)
        return ids

    def upright(ids):
        return jnp.broadcast_to(ids, (LANES, LANES)).T

    row_lines = [joined(row_ids, g) for g in range(nc // per)]
    width = min(LANES, range_len)
    base = (me_q * range_len).astype(F32)
    for g in range(nc // per):
        local = upright(row_lines[g] - base)[:, :width]
        column = iota((LANES, width), 1).astype(F32)
        onehot = jnp.concatenate(
            [
                jnp.where(local == column + float(c * width), 1.0, 0.0).astype(BF)
                for c in range(range_len // width)
            ],
            axis=1,
        )
        taken = jnp.dot(onehot, ub[...], preferred_element_type=F32).astype(BF)
        for j in range(per):
            for r in range(2):
                picks_out[g * per + j, r * slots : (r + 1) * slots, :] = taken[
                    j * slots : (j + 1) * slots, r * LANES : (r + 1) * LANES
                ]
    picks_copies = send_over_col(1, lambda peer: picks_out.at[peer], picks_in.at[me_q])
    picks_in[me_q] = picks_out[me_q]

    for s in range(nc // per):
        sub = upright(row_lines[s])
        sub_full[s * LANES : (s + 1) * LANES, :] = sub
        for t in range(nc // per):
            line = row_lines[t]
            m_full[s * LANES : (s + 1) * LANES, t * LANES : (t + 1) * LANES] = jnp.where(
                (sub == line) & (line >= 0.0), 1.0, 0.0
            ).astype(BF)
    own_rows = pl.ds(pl.multiple_of(me_q * slots, slots), slots)
    m_row = m_full[own_rows, :]
    row_live = sub_full[own_rows, :] >= 0.0

    for load in load_tiles:
        load.wait()

    def turn(first, last):
        for k in range(first, last):
            for i in range(2):
                lanes = slice(i * LANES, (i + 1) * LANES)
                tt[k * LANES : (k + 1) * LANES, lanes] = (
                    tiles_v[k, :, lanes].astype(F32).T.astype(BF)
                )

    turn(0, half // 2)
    stacked = tiles_v[...].reshape(half * LANES, 2 * LANES)

    def over_row(phase, buffer, r, values, blocks):
        own = diagonal_dot(values, blocks, slots).astype(BF)
        buffer[r, me_p] = own
        return own, send_over_row(phase + r, buffer.at[r, me_p])

    def over_col(phase, buffer, r, values, blocks):
        own = diagonal_dot(values, blocks, slots).astype(BF)
        buffer[r, me_q] = own
        return own, send_over_col(
            phase + r, lambda peer: buffer.at[r, me_q], buffer.at[r, me_q]
        )

    def total(matches, buffer, r):
        return jnp.dot(
            matches, buffer[r].reshape(-1, LANES), preferred_element_type=F32
        )

    def inner(own, summed, live):
        return total_of(jnp.where(live, own.astype(F32) * summed, 0.0))

    arrived(picks_copies)
    c0_sent = []
    for r in range(2):
        u0 = picks_in[0, r * slots : (r + 1) * slots, :].astype(F32)
        for j in range(1, nc):
            u0 = u0 + picks_in[j, r * slots : (r + 1) * slots, :].astype(F32)
        c0_sent.append(over_row(1, c0, r, u0, stacked))

    turn(half // 2, half)
    arrived(col_ids_copies)
    sub_col = upright(col_ids[me_p])[:slots]
    col_live = sub_col >= 0.0
    col_lines = [joined(col_ids, g) for g in range(nr // per)]
    for s in range(nr // per):
        line = col_lines[s]
        m_col[:, s * LANES : (s + 1) * LANES] = jnp.where(
            (sub_col == line) & (line >= 0.0), 1.0, 0.0
        ).astype(BF)
    col_base = (me_p * range_len).astype(F32)
    chunk = min(256, range_len)
    for start in range(0, range_len, chunk):
        number = (iota((chunk, LANES), 0) + start).astype(F32)
        for s in range(nr // per):
            place[start : start + chunk, s * LANES : (s + 1) * LANES] = jnp.where(
                number == col_lines[s] - col_base, 1.0, 0.0
            ).astype(BF)

    def put(buffer, target):
        both = jnp.concatenate([buffer[r].reshape(nr * slots, LANES) for r in range(2)], axis=1)
        for start in range(0, range_len, chunk):
            target[start : start + chunk, :] = jnp.dot(
                place[start : start + chunk, :], both, preferred_element_type=F32
            )

    g0, d0_sent = [], []
    for r in range(2):
        arrived(c0_sent[r][1])
        g0.append(total(m_col[...], c0, r))
        d0_sent.append(over_col(2, d0, r, g0[r], tt[...]))
    gg = [inner(c0_sent[r][0], g0[r], col_live) for r in range(2)]

    f0, c1_sent = [], []
    for r in range(2):
        arrived(d0_sent[r][1])
        f0.append(total(m_row, d0, r))
        c1_sent.append(over_row(3, c1, r, f0[r], stacked))
    ff = [inner(d0_sent[r][0], f0[r], row_live) for r in range(2)]
    put(c0, placed0)

    g1, d1_sent = [], []
    for r in range(2):
        arrived(c1_sent[r][1])
        g1.append(total(m_col[...], c1, r))
        d1_sent.append(over_col(4, d1, r, g1[r], tt[...]))
    hh = [inner(c1_sent[r][0], g1[r], col_live) for r in range(2)]

    stats = jnp.zeros((1, LANES), F32)
    for s, pair in enumerate((squares, gg, ff, hh)):
        for r in range(2):
            stats = jnp.where(lane == 2 * s + r, pair[r], stats)
    stats_col[me_q] = stats
    stats_col_copies = send_over_col(6, lambda peer: stats_col.at[me_q], stats_col.at[me_q])

    full_live = sub_full[...] >= 0.0
    ee = []
    for r in range(2):
        arrived(d1_sent[r][1])
        f1 = total(m_full[...], d1, r)
        ee.append(inner(d1[r].reshape(nc * slots, LANES), f1, full_live))
    arrived(stats_col_copies)
    group = jnp.sum(stats_col[...], axis=0)
    for r in range(2):
        group = jnp.where(lane == 8 + r, ee[r], group)
    stats_row[me_p] = group
    stats_row_copies = send_over_row(5, stats_row.at[me_p])
    put(c1, placed1)
    arrived(stats_row_copies)
    whole = jnp.sum(stats_row[...], axis=0)

    uu, gg, ff, hh, ee = [whole] + [pltpu.roll(whole, LANES - 2 * s, 1) for s in range(1, 5)]

    def norm(square):
        return jnp.sqrt(jnp.maximum(square, 0.0) + EPS)

    beta0 = norm(uu)
    alpha0 = norm(gg / (beta0 * beta0))
    a = 1.0 / (beta0 * alpha0)
    b = alpha0 / beta0
    beta1 = norm(a * a * ff - 2.0 * (a * b) * gg + b * b * uu)
    rho0 = jnp.sqrt(alpha0 * alpha0 + beta1 * beta1)
    cosine = alpha0 / rho0
    sine = beta1 / rho0
    phi0 = cosine * beta0
    phi_bar = sine * beta0
    x = a / beta1
    y = -(b / beta1 + beta1 * a)
    alpha1 = norm(x * x * hh + 2.0 * (x * y) * ff + y * y * gg)
    theta = sine * alpha1
    rho_bar = -cosine * alpha1
    e = x / alpha1
    h = y / alpha1 - (alpha1 / beta1) * a
    w = (alpha1 / beta1) * b
    beta2 = norm(
        e * e * ee + h * h * ff + w * w * uu
        + 2.0 * (e * h) * hh + 2.0 * (e * w) * ff + 2.0 * (h * w) * gg
    )
    rho1 = jnp.sqrt(rho_bar * rho_bar + beta2 * beta2)
    phi1 = (rho_bar / rho1) * phi_bar
    phi_ref[...] = ((beta2 / rho1) * phi_bar)[:, 0:2]
    on_g1 = (phi1 / rho1) * e
    on_g0 = (phi0 / rho0) * a + (phi1 / rho1) * (y / alpha1 - (theta / rho0) * a)

    for start in range(0, range_len, chunk):
        here = slice(start, start + chunk)
        for r in range(2):
            lanes = slice(r * LANES, (r + 1) * LANES)
            out_ref[pl.ds(2 * start + r, chunk, stride=2), :] = (
                placed0[here, lanes] * on_g0[:, r : r + 1]
                + placed1[here, lanes] * on_g1[:, r : r + 1]
            )

    for copy in sent:
        copy.wait_send()


def on_device(nr, nc, tiles, coords, counts, rhs):
    slots, block = tiles.shape[2], tiles.shape[3]
    range_len = rhs.shape[1] // block
    piece = rhs.reshape(2, range_len, block).transpose(1, 0, 2).reshape(2 * range_len, block)
    dma = pltpu.SemaphoreType.DMA
    placed, phi = pl.pallas_call(
        functools.partial(solver, nr, nc, slots, range_len),
        out_shape=(
            jax.ShapeDtypeStruct((2 * range_len, block), F32),
            jax.ShapeDtypeStruct((1, 2), F32),
        ),
        in_specs=[
            pl.BlockSpec(memory_space=pltpu.HBM),
            pl.BlockSpec(memory_space=pltpu.SMEM),
            pl.BlockSpec(memory_space=pltpu.HBM),
            pl.BlockSpec(memory_space=pltpu.HBM),
        ],
        out_specs=(
            pl.BlockSpec(memory_space=pltpu.VMEM),
            pl.BlockSpec(memory_space=pltpu.VMEM),
        ),
        scratch_shapes=[
            pltpu.VMEM((2, slots), jnp.int32),
            pltpu.VMEM((2 * range_len, block), F32),
            pltpu.VMEM((range_len, 2 * block), BF),
            pltpu.VMEM((slots // 2, block, 2 * block), BF),
            pltpu.VMEM((slots // 2 * block, 2 * block), BF),
            pltpu.VMEM((nc, 1, LANES), F32),
            pltpu.VMEM((nr, 1, LANES), F32),
            pltpu.VMEM((nc, 2 * slots, block), BF),
            pltpu.VMEM((nc, 2 * slots, block), BF),
            pltpu.VMEM((2, nr, slots, block), BF),
            pltpu.VMEM((2, nr, slots, block), BF),
            pltpu.VMEM((2, nc, slots, block), BF),
            pltpu.VMEM((2, nc, slots, block), BF),
            pltpu.VMEM((nc, 1, LANES), F32),
            pltpu.VMEM((nr, 1, LANES), F32),
            pltpu.VMEM((slots, nr * slots), BF),
            pltpu.VMEM((nc * slots, nc * slots), BF),
            pltpu.VMEM((nc * slots, LANES), F32),
            pltpu.VMEM((range_len, nr * slots), BF),
            pltpu.VMEM((range_len, 2 * block), F32),
            pltpu.VMEM((range_len, 2 * block), F32),
            dma((4,)),
            dma((7, nc - 1)),
            dma((7, nc - 1)),
            dma((6, nr - 1)),
            dma((6, nr - 1)),
        ],
        compiler_params=pltpu.CompilerParams(
            collective_id=0, has_side_effects=True, vmem_limit_bytes=48 * 1024 * 1024
        ),
    )(
        pltpu.with_memory_space_constraint(coords[0, 0].T, pltpu.HBM),
        counts,
        pltpu.with_memory_space_constraint(tiles[0, 0], pltpu.HBM),
        pltpu.with_memory_space_constraint(piece, pltpu.HBM),
    )
    answer = placed.reshape(range_len, 2, block).transpose(1, 0, 2).reshape(2, range_len * block)
    return answer, phi[0]


def solution(mesh):
    nr, nc = mesh.shape["row"], mesh.shape["col"]
    return jax.shard_map(
        functools.partial(on_device, nr, nc),
        mesh=mesh,
        in_specs=(
            P("row", "col", None, None, None),
            P("row", "col", None, None),
            P("row", "col"),
            P(None, ("row", "col")),
        ),
        out_specs=(P(None, ("col", "row")), P()),
        check_vma=False,
    )
```

time: 36.6 us -> 36.1 us (0.986)
  Pallas kernels: 33.7 us -> 33.2 us
    pallas_call x1, Pallas kernels: 33.7 us -> 33.2 us  [on_device(): pl.pallas_call(functools.partial(solver, nr, nc, slots, range_len), out_s...]
where the time goes in v4:
time: 36.1 us; the launch traced here: 36 us
  Pallas kernels  33.2 us (92%)
  local copies, waits for them, and re-layouts  1.48 us (4%)
  between operations  1.28 us (4%)
    pallas_call x1, Pallas kernels, on_device(): pl.pallas_call(functools.partial(solver, nr, nc, slots, range_len), out_s...  33.2 us
    unnamed x2, local copies, waits for them, and re-layouts  1.48 us

profile of v4, /device:TPU:0, one launch (start us, length us, event | category | flops | bytes accessed | tf_op | source)
XLA Modules:
  0.0 36.0 jit_solution(18085503436587092795)
XLA Ops:
  1.3 33.2 %shard_map.59 = (f32[2048,128]{1,0:T(8,128)S(1)}, f32[1,2]{1,0:T(1,128)S(1)}) custom-call(s32[2,32]{1,0:T(2,128)} %bitcast.19, s32[1,1]{1,0:T(1,128)S(6)} %copy.10.counts, bf16[32,128,128]{2,1,0:T(8,128)(2,1)} %bitcast.17, f32[2048,128]{1,0:T(8,128)} %bitcast.18), custom_call_target="tpu_custom_call" | custom-call | tf_op jit(solution)/shard_map/pallas_call | solution.py:357
  34.5 1.0 %copy.11 = f32[2,131072]{1,0:T(2,128)} copy(f32[2,131072]{1,0:T(2,128)S(1)} %bitcast.15) | data formatting | bytes 2097152
  35.4 0.5 %copy.12 = f32[2]{0:T(128)} copy(f32[2]{0:T(128)S(1)} %bitcast.16) | data formatting | bytes 16

commit v5 on v4

--- a/solution.py
+++ b/solution.py
@@ -100,7 +100,7 @@
 
     def send_over_col(phase, source, mine):
         copies = []
-        for o in range(1, nc):
+        for o in sorted(range(1, nc), key=lambda o: abs(2 * o - nc)):
             copy = pltpu.make_async_remote_copy(
                 src_ref=source(lax.rem(me_q + o, nc)),
                 dst_ref=mine,
@@ -116,7 +116,7 @@
 
     def send_over_row(phase, mine):
         copies = []
-        for o in range(1, nr):
+        for o in sorted(range(1, nr), key=lambda o: abs(2 * o - nr)):
             copy = pltpu.make_async_remote_copy(
                 src_ref=mine,
                 dst_ref=mine,
@@ -198,10 +198,10 @@
             for i in range(2):
                 lanes = slice(i * LANES, (i + 1) * LANES)
                 tt[k * LANES : (k + 1) * LANES, lanes] = (
-                    tiles_v[k, :, lanes].astype(F32).T.astype(BF)
+                    tiles_v[k, :, lanes].T
                 )
 
-    turn(0, half // 2)
+    turn(0, half // 4)
     stacked = tiles_v[...].reshape(half * LANES, 2 * LANES)
 
     def over_row(phase, buffer, r, values, blocks):
@@ -232,7 +232,7 @@
             u0 = u0 + picks_in[j, r * slots : (r + 1) * slots, :].astype(F32)
         c0_sent.append(over_row(1, c0, r, u0, stacked))
 
-    turn(half // 2, half)
+    turn(half // 4, half)
     arrived(col_ids_copies)
     sub_col = upright(col_ids[me_p])[:slots]
     col_live = sub_col >= 0.0
@@ -242,35 +242,35 @@
         m_col[:, s * LANES : (s + 1) * LANES] = jnp.where(
             (sub_col == line) & (line >= 0.0), 1.0, 0.0
         ).astype(BF)
+    chunk = min(256, range_len)
+
+    def put(buffer, target):
+        both = jnp.concatenate([buffer[r].reshape(nr * slots, LANES) for r in range(2)], axis=1)
+        for start in range(0, range_len, chunk):
+            target[start : start + chunk, :] = jnp.dot(
+                place[start : start + chunk, :], both, preferred_element_type=F32
+            )
+
+    g0, d0_sent = [], []
+    for r in range(2):
+        arrived(c0_sent[r][1])
+        g0.append(total(m_col[...], c0, r))
+        d0_sent.append(over_col(2, d0, r, g0[r], tt[...]))
+    gg = [inner(c0_sent[r][0], g0[r], col_live) for r in range(2)]
+
+    f0, c1_sent = [], []
+    for r in range(2):
+        arrived(d0_sent[r][1])
+        f0.append(total(m_row, d0, r))
+        c1_sent.append(over_row(3, c1, r, f0[r], stacked))
+    ff = [inner(d0_sent[r][0], f0[r], row_live) for r in range(2)]
     col_base = (me_p * range_len).astype(F32)
-    chunk = min(256, range_len)
     for start in range(0, range_len, chunk):
         number = (iota((chunk, LANES), 0) + start).astype(F32)
         for s in range(nr // per):
             place[start : start + chunk, s * LANES : (s + 1) * LANES] = jnp.where(
                 number == col_lines[s] - col_base, 1.0, 0.0
             ).astype(BF)
-
-    def put(buffer, target):
-        both = jnp.concatenate([buffer[r].reshape(nr * slots, LANES) for r in range(2)], axis=1)
-        for start in range(0, range_len, chunk):
-            target[start : start + chunk, :] = jnp.dot(
-                place[start : start + chunk, :], both, preferred_element_type=F32
-            )
-
-    g0, d0_sent = [], []
-    for r in range(2):
-        arrived(c0_sent[r][1])
-        g0.append(total(m_col[...], c0, r))
-        d0_sent.append(over_col(2, d0, r, g0[r], tt[...]))
-    gg = [inner(c0_sent[r][0], g0[r], col_live) for r in range(2)]
-
-    f0, c1_sent = [], []
-    for r in range(2):
-        arrived(d0_sent[r][1])
-        f0.append(total(m_row, d0, r))
-        c1_sent.append(over_row(3, c1, r, f0[r], stacked))
-    ff = [inner(d0_sent[r][0], f0[r], row_live) for r in range(2)]
     put(c0, placed0)
 
     g1, d1_sent = [], []
@@ -298,8 +298,11 @@
     for r in range(2):
         group = jnp.where(lane == 8 + r, ee[r], group)
     stats_row[me_p] = group
+    earlier = list(sent)
     stats_row_copies = send_over_row(5, stats_row.at[me_p])
     put(c1, placed1)
+    for copy in earlier:
+        copy.wait_send()
     arrived(stats_row_copies)
     whole = jnp.sum(stats_row[...], axis=0)
 
@@ -345,7 +348,7 @@
                 + placed1[here, lanes] * on_g1[:, r : r + 1]
             )
 
-    for copy in sent:
+    for copy in stats_row_copies:
         copy.wait_send()
 
 

time: 36.1 us -> 36.4 us (level)
  no operation moved by 1% of the time
where the time goes in v5:
time: 36.4 us; the launch traced here: 36.3 us
  Pallas kernels  33.5 us (92%)
  local copies, waits for them, and re-layouts  1.48 us (4%)
  between operations  1.28 us (4%)
    pallas_call x1, Pallas kernels, on_device(): pl.pallas_call(functools.partial(solver, nr, nc, slots, range_len), out_s...  33.5 us
    unnamed x2, local copies, waits for them, and re-layouts  1.48 us

profile of v5, /device:TPU:0, one launch (start us, length us, event | category | flops | bytes accessed | tf_op | source)
XLA Modules:
  0.0 36.3 jit_solution(3908787152484771830)
XLA Ops:
  1.3 33.5 %shard_map.59 = (f32[2048,128]{1,0:T(8,128)S(1)}, f32[1,2]{1,0:T(1,128)S(1)}) custom-call(s32[2,32]{1,0:T(2,128)} %bitcast.19, s32[1,1]{1,0:T(1,128)S(6)} %copy.10.counts, bf16[32,128,128]{2,1,0:T(8,128)(2,1)} %bitcast.17, f32[2048,128]{1,0:T(8,128)} %bitcast.18), custom_call_target="tpu_custom_call" | custom-call | tf_op jit(solution)/shard_map/pallas_call | solution.py:360
  34.8 1.0 %copy.11 = f32[2,131072]{1,0:T(2,128)} copy(f32[2,131072]{1,0:T(2,128)S(1)} %bitcast.15) | data formatting | bytes 2097152
  35.8 0.5 %copy.12 = f32[2]{0:T(128)} copy(f32[2]{0:T(128)S(1)} %bitcast.16) | data formatting | bytes 16

commit v6 on v5

--- a/solution.py
+++ b/solution.py
@@ -19,23 +19,28 @@
 
 def diagonal_dot(values, stacked, slots):
     group, half = 8, slots // 2
-    row_slot = iota((2 * group, LANES), 0) % group
-    first, second = [], []
+    row_slot = iota((4 * group, LANES), 0) % group
+    parts = []
     for start in range(0, half, group):
-        pair = jnp.concatenate(
-            [values[start : start + group], values[half + start : half + start + group]], axis=0
+        quad = jnp.concatenate(
+            [v[i + start : i + start + group] for v in values for i in (0, half)], axis=0
         )
         wide = jnp.concatenate(
-            [jnp.where(row_slot == k, pair, 0.0).astype(BF) for k in range(group)], axis=1
-        )
-        result = jnp.dot(
-            wide,
-            stacked[start * LANES : (start + group) * LANES],
-            preferred_element_type=F32,
-        )
-        first.append(result[:group, :LANES])
-        second.append(result[group:, LANES:])
-    return jnp.concatenate(first + second, axis=0)
+            [jnp.where(row_slot == k, quad, 0.0).astype(BF) for k in range(group)], axis=1
+        )
+        parts.append(
+            jnp.dot(
+                wide,
+                stacked[start * LANES : (start + group) * LANES],
+                preferred_element_type=F32,
+            )
+        )
+    pieces = []
+    for r in range(2):
+        for i in range(2):
+            at = (2 * r + i) * group
+            pieces += [p[at : at + group, i * LANES : (i + 1) * LANES] for p in parts]
+    return jnp.concatenate(pieces, axis=0)
 
 
 def total_of(products):
@@ -204,33 +209,40 @@
     turn(0, half // 4)
     stacked = tiles_v[...].reshape(half * LANES, 2 * LANES)
 
-    def over_row(phase, buffer, r, values, blocks):
+    def over_row(phase, buffer, values, blocks):
         own = diagonal_dot(values, blocks, slots).astype(BF)
-        buffer[r, me_p] = own
-        return own, send_over_row(phase + r, buffer.at[r, me_p])
-
-    def over_col(phase, buffer, r, values, blocks):
+        buffer[me_p] = own
+        return own, send_over_row(phase, buffer.at[me_p])
+
+    def over_col(phase, buffer, values, blocks):
         own = diagonal_dot(values, blocks, slots).astype(BF)
-        buffer[r, me_q] = own
-        return own, send_over_col(
-            phase + r, lambda peer: buffer.at[r, me_q], buffer.at[r, me_q]
-        )
-
-    def total(matches, buffer, r):
-        return jnp.dot(
-            matches, buffer[r].reshape(-1, LANES), preferred_element_type=F32
-        )
+        buffer[me_q] = own
+        return own, send_over_col(phase, lambda peer: buffer.at[me_q], buffer.at[me_q])
+
+    def of(buffer, r):
+        return buffer[:, r * slots : (r + 1) * slots, :].reshape(-1, LANES)
+
+    def beside(buffer):
+        return jnp.concatenate([of(buffer, r) for r in range(2)], axis=1)
+
+    def total(matches, buffer):
+        both = jnp.dot(matches, beside(buffer), preferred_element_type=F32)
+        return [both[:, r * LANES : (r + 1) * LANES] for r in range(2)]
 
     def inner(own, summed, live):
         return total_of(jnp.where(live, own.astype(F32) * summed, 0.0))
 
+    def inners(own, summed, live):
+        return [inner(own[r * slots : (r + 1) * slots], summed[r], live) for r in range(2)]
+
     arrived(picks_copies)
-    c0_sent = []
+    u0 = []
     for r in range(2):
-        u0 = picks_in[0, r * slots : (r + 1) * slots, :].astype(F32)
+        part = picks_in[0, r * slots : (r + 1) * slots, :].astype(F32)
         for j in range(1, nc):
-            u0 = u0 + picks_in[j, r * slots : (r + 1) * slots, :].astype(F32)
-        c0_sent.append(over_row(1, c0, r, u0, stacked))
+            part = part + picks_in[j, r * slots : (r + 1) * slots, :].astype(F32)
+        u0.append(part)
+    c0_own, c0_copies = over_row(1, c0, u0, stacked)
 
     turn(half // 4, half)
     arrived(col_ids_copies)
@@ -245,25 +257,21 @@
     chunk = min(256, range_len)
 
     def put(buffer, target):
-        both = jnp.concatenate([buffer[r].reshape(nr * slots, LANES) for r in range(2)], axis=1)
+        both = beside(buffer)
         for start in range(0, range_len, chunk):
             target[start : start + chunk, :] = jnp.dot(
                 place[start : start + chunk, :], both, preferred_element_type=F32
             )
 
-    g0, d0_sent = [], []
-    for r in range(2):
-        arrived(c0_sent[r][1])
-        g0.append(total(m_col[...], c0, r))
-        d0_sent.append(over_col(2, d0, r, g0[r], tt[...]))
-    gg = [inner(c0_sent[r][0], g0[r], col_live) for r in range(2)]
-
-    f0, c1_sent = [], []
-    for r in range(2):
-        arrived(d0_sent[r][1])
-        f0.append(total(m_row, d0, r))
-        c1_sent.append(over_row(3, c1, r, f0[r], stacked))
-    ff = [inner(d0_sent[r][0], f0[r], row_live) for r in range(2)]
+    arrived(c0_copies)
+    g0 = total(m_col[...], c0)
+    d0_own, d0_copies = over_col(2, d0, g0, tt[...])
+    gg = inners(c0_own, g0, col_live)
+
+    arrived(d0_copies)
+    f0 = total(m_row, d0)
+    c1_own, c1_copies = over_row(3, c1, f0, stacked)
+    ff = inners(d0_own, f0, row_live)
     col_base = (me_p * range_len).astype(F32)
     for start in range(0, range_len, chunk):
         number = (iota((chunk, LANES), 0) + start).astype(F32)
@@ -273,12 +281,10 @@
             ).astype(BF)
     put(c0, placed0)
 
-    g1, d1_sent = [], []
-    for r in range(2):
-        arrived(c1_sent[r][1])
-        g1.append(total(m_col[...], c1, r))
-        d1_sent.append(over_col(4, d1, r, g1[r], tt[...]))
-    hh = [inner(c1_sent[r][0], g1[r], col_live) for r in range(2)]
+    arrived(c1_copies)
+    g1 = total(m_col[...], c1)
+    d1_own, d1_copies = over_col(4, d1, g1, tt[...])
+    hh = inners(c1_own, g1, col_live)
 
     stats = jnp.zeros((1, LANES), F32)
     for s, pair in enumerate((squares, gg, ff, hh)):
@@ -288,11 +294,9 @@
     stats_col_copies = send_over_col(6, lambda peer: stats_col.at[me_q], stats_col.at[me_q])
 
     full_live = sub_full[...] >= 0.0
-    ee = []
-    for r in range(2):
-        arrived(d1_sent[r][1])
-        f1 = total(m_full[...], d1, r)
-        ee.append(inner(d1[r].reshape(nc * slots, LANES), f1, full_live))
+    arrived(d1_copies)
+    f1 = total(m_full[...], d1)
+    ee = [inner(of(d1, r), f1[r], full_live) for r in range(2)]
     arrived(stats_col_copies)
     group = jnp.sum(stats_col[...], axis=0)
     for r in range(2):
@@ -383,10 +387,10 @@
             pltpu.VMEM((nr, 1, LANES), F32),
             pltpu.VMEM((nc, 2 * slots, block), BF),
             pltpu.VMEM((nc, 2 * slots, block), BF),
-            pltpu.VMEM((2, nr, slots, block), BF),
-            pltpu.VMEM((2, nr, slots, block), BF),
-            pltpu.VMEM((2, nc, slots, block), BF),
-            pltpu.VMEM((2, nc, slots, block), BF),
+            pltpu.VMEM((nr, 2 * slots, block), BF),
+            pltpu.VMEM((nr, 2 * slots, block), BF),
+            pltpu.VMEM((nc, 2 * slots, block), BF),
+            pltpu.VMEM((nc, 2 * slots, block), BF),
             pltpu.VMEM((nc, 1, LANES), F32),
             pltpu.VMEM((nr, 1, LANES), F32),
             pltpu.VMEM((slots, nr * slots), BF),

time: 36.4 us -> 37.4 us (1.027)
  Pallas kernels: 33.5 us -> 34.4 us
    pallas_call x1, Pallas kernels: 33.5 us -> 34.4 us  [on_device(): pl.pallas_call(functools.partial(solver, nr, nc, slots, range_len), out_s...]
where the time goes in v6:
time: 37.4 us; the launch traced here: 37.2 us
  Pallas kernels  34.4 us (92%)
  local copies, waits for them, and re-layouts  1.48 us (4%)
  between operations  1.28 us (3%)
    pallas_call x1, Pallas kernels, on_device(): pl.pallas_call(functools.partial(solver, nr, nc, slots, range_len), out_s...  34.4 us
    unnamed x2, local copies, waits for them, and re-layouts  1.48 us

profile of v6, /device:TPU:0, one launch (start us, length us, event | category | flops | bytes accessed | tf_op | source)
XLA Modules:
  0.0 37.2 jit_solution(3552644405016257389)
XLA Ops:
  1.3 34.4 %shard_map.59 = (f32[2048,128]{1,0:T(8,128)S(1)}, f32[1,2]{1,0:T(1,128)S(1)}) custom-call(s32[2,32]{1,0:T(2,128)} %bitcast.19, s32[1,1]{1,0:T(1,128)S(6)} %copy.10.counts, bf16[32,128,128]{2,1,0:T(8,128)(2,1)} %bitcast.17, f32[2048,128]{1,0:T(8,128)} %bitcast.18), custom_call_target="tpu_custom_call" | custom-call | tf_op jit(solution)/shard_map/pallas_call | solution.py:364
  35.7 1.0 %copy.11 = f32[2,131072]{1,0:T(2,128)} copy(f32[2,131072]{1,0:T(2,128)S(1)} %bitcast.15) | data formatting | bytes 2097152
  36.7 0.5 %copy.12 = f32[2]{0:T(128)} copy(f32[2]{0:T(128)S(1)} %bitcast.16) | data formatting | bytes 16

commit v7 on v4

--- a/solution.py
+++ b/solution.py
@@ -298,8 +298,11 @@
     for r in range(2):
         group = jnp.where(lane == 8 + r, ee[r], group)
     stats_row[me_p] = group
+    earlier = list(sent)
     stats_row_copies = send_over_row(5, stats_row.at[me_p])
     put(c1, placed1)
+    for copy in earlier:
+        copy.wait_send()
     arrived(stats_row_copies)
     whole = jnp.sum(stats_row[...], axis=0)
 
@@ -345,7 +348,7 @@
                 + placed1[here, lanes] * on_g1[:, r : r + 1]
             )
 
-    for copy in sent:
+    for copy in stats_row_copies:
         copy.wait_send()
 
 

time: 36.1 us -> 36 us (level)
  no operation moved by 1% of the time
where the time goes in v7:
time: 36 us; the launch traced here: 35.9 us
  Pallas kernels  33.1 us (92%)
  local copies, waits for them, and re-layouts  1.48 us (4%)
  between operations  1.28 us (4%)
    pallas_call x1, Pallas kernels, on_device(): pl.pallas_call(functools.partial(solver, nr, nc, slots, range_len), out_s...  33.1 us
    unnamed x2, local copies, waits for them, and re-layouts  1.48 us

profile of v7, /device:TPU:0, one launch (start us, length us, event | category | flops | bytes accessed | tf_op | source)
XLA Modules:
  0.0 35.9 jit_solution(16941870019891014277)
XLA Ops:
  1.3 33.1 %shard_map.59 = (f32[2048,128]{1,0:T(8,128)S(1)}, f32[1,2]{1,0:T(1,128)S(1)}) custom-call(s32[2,32]{1,0:T(2,128)} %bitcast.19, s32[1,1]{1,0:T(1,128)S(6)} %copy.10.counts, bf16[32,128,128]{2,1,0:T(8,128)(2,1)} %bitcast.17, f32[2048,128]{1,0:T(8,128)} %bitcast.18), custom_call_target="tpu_custom_call" | custom-call | tf_op jit(solution)/shard_map/pallas_call | solution.py:360
  34.4 1.0 %copy.11 = f32[2,131072]{1,0:T(2,128)} copy(f32[2,131072]{1,0:T(2,128)S(1)} %bitcast.15) | data formatting | bytes 2097152
  35.4 0.5 %copy.12 = f32[2]{0:T(128)} copy(f32[2]{0:T(128)S(1)} %bitcast.16) | data formatting | bytes 16
